TPU v7x, 512 devices: a whole 4x4x16 slice. The times are simulated.
512 devices in a mesh: ctx: 64 (over z, x), head: 8 (over y, core).
Axes of the slice: x: 4, y: 4, z: 16, core: 2. Of those that a mesh axis runs over, the one named last changes fastest.
Arguments:
- queries: float32 [32768, 2048], P('ctx', 'head'), may hold values from -1024 to 1024
- keys: float32 [32768, 128], P('ctx'), may hold values from -1024 to 1024
- values: float32 [32768, 128], P('ctx'), may hold values from -6 to 6
- cotangent: float32 [32768, 2048], P('ctx', 'head'), may hold values from -384 to 384
- source_ids: int32 [32768], P('ctx'), may hold values from 0 to 63
- source_weights: float32 [64], replicated, may hold values from 0.25 to 4
- q_feature: float32 [16, 128, 128], P('head'), may hold values from -4 to 4
- k_feature: float32 [128, 128], replicated, may hold values from -4 to 4
Outputs:
- grad_queries: float32 [32768, 2048], P('ctx', 'head')
- grad_keys: float32 [32768, 128], P(('ctx', 'head'))
- grad_values: float32 [32768, 128], P(('ctx', 'head'))
- grad_q_feature: float32 [16, 128, 128], P('head')
- grad_k_feature: float32 [128, 128], replicated
All inputs are finite; a program needn't handle non-finite values.
Results may differ from a plain program's by a relative error of at most 0.0015.
Values sent between devices are 32-bit elements; how exact they have to be, the bound alone decides.
A program may use at most 64 MiB of HBM per device.

v0:
```python
import jax
import jax.numpy as jnp
from jax import lax
from jax.sharding import PartitionSpec as P


def entering(value, axis, join, neutral, backward):
    count, mine = (lax.axis_size(axis), lax.axis_index(axis))
    pieces = jax.tree.map(lambda part: lax.all_gather(part, axis), value)
    if backward:
        pieces = jax.tree.map(lambda part: part[::-1], pieces)
        mine = count - 1 - mine
    total = jax.tree.map(
        lambda part, zero: jnp.full_like(part, 0) + jnp.asarray(zero, part.dtype), value, neutral
    )

    def turn(position, total):
        longer = join(total, jax.tree.map(lambda part: part[position], pieces))
        return jax.tree.map(lambda new, old: jnp.where(position < mine, new, old), longer, total)

    return lax.fori_loop(0, count - 1, turn, total)


def matmul(left, right):
    return jnp.dot(left, right, precision=lax.Precision.HIGHEST, preferred_element_type=jnp.float32)


def product(form, left, right):
    return jnp.einsum(
        form, left, right, precision=lax.Precision.HIGHEST, preferred_element_type=jnp.float32
    )


def feature_map(inputs, weight):
    logits = matmul(inputs, weight)
    upper = jax.nn.softmax(logits, axis=-1)
    lower = jax.nn.softmax(-logits, axis=-1)
    return (jnp.concatenate([upper, lower], axis=-1), upper, lower)


def feature_back(inputs, weight, upper, lower, grad_feat):
    half = upper.shape[-1]
    grad_upper = grad_feat[:, :half]
    grad_lower = grad_feat[:, half:]
    grad_logits = upper * (grad_upper - jnp.sum(upper * grad_upper, axis=-1, keepdims=True))
    grad_logits = grad_logits - lower * (
        grad_lower - jnp.sum(lower * grad_lower, axis=-1, keepdims=True)
    )
    return (matmul(grad_logits, weight.T), matmul(inputs.T, grad_logits))


def causal_mask(count):
    row_index = lax.broadcasted_iota(jnp.int32, (count, count), 0)
    col_index = lax.broadcasted_iota(jnp.int32, (count, count), 1)
    return (row_index >= col_index).astype(jnp.float32)


def add_pair(earlier, later):
    return (earlier[0] + later[0], earlier[1] + later[1])


def block_terms(query_c, key_c, value_c, scaled_c, prefix, prefix_tot):
    lower_mask = causal_mask(query_c.shape[1])
    scores = product("ncf,ndf->ncd", query_c, key_c) * lower_mask
    numerator = product("ncd,nde->nce", scores, value_c) + product("ncf,nfe->nce", query_c, prefix)
    normalizer = jnp.sum(scores, axis=2) + product("ncf,nf->nc", query_c, prefix_tot)
    output = numerator / normalizer[..., None]
    grad_numer = scaled_c / normalizer[..., None]
    grad_norm = -jnp.sum(scaled_c * output, axis=2) / normalizer
    grad_scores = (product("nce,nde->ncd", grad_numer, value_c) + grad_norm[..., None]) * lower_mask
    grad_query = (
        product("ncd,ndf->ncf", grad_scores, key_c)
        + product("nce,nfe->ncf", grad_numer, prefix)
        + grad_norm[..., None] * prefix_tot[:, None, :]
    )
    grad_key = product("ncd,ncf->ndf", grad_scores, query_c)
    grad_value = product("ncd,nce->nde", scores, grad_numer)
    carried = product("ncf,nce->nfe", query_c, grad_numer)
    carried_totals = product("nc,ncf->nf", grad_norm, query_c)
    return (grad_query, grad_key, grad_value, carried, carried_totals)


def on_device(queries, keys, values, cotangent, source_ids, source_weights, q_feature, k_feature):
    head_count = q_feature.shape[0]
    width = q_feature.shape[1]
    features = 2 * q_feature.shape[2]
    rows = queries.shape[0]
    piece = min(128, rows)
    pieces = rows // piece
    source_index = lax.broadcasted_iota(jnp.int32, (1, source_weights.shape[0]), 1)
    lookup = (source_ids[:, None] == source_index).astype(jnp.float32)
    weight = jnp.sum(lookup * source_weights[None, :], axis=1)
    key_feat, key_upper, key_lower = feature_map(keys, k_feature)
    key_c = key_feat.reshape(pieces, piece, features)
    value_c = values.reshape(pieces, piece, width)
    piece_state = product("ncf,nce->nfe", key_c, value_c)
    piece_tot = jnp.sum(key_c, axis=1)
    whole_local = (jnp.sum(piece_state, axis=0), jnp.sum(piece_tot, axis=0))
    whole_zero = (jnp.zeros((features, width), jnp.float32), jnp.zeros((features,), jnp.float32))
    earlier, earlier_totals = entering(
        (whole_local[0], whole_local[1]), "ctx", add_pair, whole_zero, False
    )
    prefix = jnp.cumsum(piece_state, axis=0) - piece_state + earlier[None]
    prefix_tot = jnp.cumsum(piece_tot, axis=0) - piece_tot + earlier_totals[None]
    grad_keyfeat = jnp.zeros(key_feat.shape, jnp.float32)
    grad_vals = jnp.zeros(values.shape, jnp.float32)
    piece_carried = jnp.zeros((pieces, features, width), jnp.float32)
    piece_carried_tot = jnp.zeros((pieces, features), jnp.float32)
    query_grads = []
    weight_grads = []
    for head in range(head_count):
        query_head = queries[:, head * width : (head + 1) * width]
        query_feat, query_upper, query_lower = feature_map(query_head, q_feature[head])
        scaled = cotangent[:, head * width : (head + 1) * width] * weight[:, None]
        grad_query, grad_key, grad_value, carried, carried_totals = block_terms(
            query_feat.reshape(pieces, piece, features),
            key_c,
            value_c,
            scaled.reshape(pieces, piece, width),
            prefix,
            prefix_tot,
        )
        grad_head, grad_weight = feature_back(
            query_head,
            q_feature[head],
            query_upper,
            query_lower,
            grad_query.reshape(rows, features),
        )
        query_grads.append(grad_head)
        weight_grads.append(grad_weight)
        grad_keyfeat = grad_keyfeat + grad_key.reshape(rows, features)
        grad_vals = grad_vals + grad_value.reshape(rows, width)
        piece_carried = piece_carried + carried
        piece_carried_tot = piece_carried_tot + carried_totals
    carried_all = jnp.sum(piece_carried, axis=0)
    carried_tot = jnp.sum(piece_carried_tot, axis=0)
    inner_later = carried_all[None] - jnp.cumsum(piece_carried, axis=0)
    inner_tot = carried_tot[None] - jnp.cumsum(piece_carried_tot, axis=0)
    grad_keyfeat = grad_keyfeat + (
        product("nce,nfe->ncf", value_c, inner_later) + inner_tot[:, None, :]
    ).reshape(rows, features)
    grad_vals = grad_vals + product("ncf,nfe->nce", key_c, inner_later).reshape(rows, width)
    later, later_tot = entering((carried_all, carried_tot), "ctx", add_pair, whole_zero, True)
    grad_keyfeat = grad_keyfeat + matmul(values, later.T) + later_tot[None, :]
    grad_vals = grad_vals + matmul(key_feat, later)
    grad_key_part, grad_kweight = feature_back(keys, k_feature, key_upper, key_lower, grad_keyfeat)
    grad_keys, grad_values = (
        lax.psum_scatter(grad_key_part, "head", scatter_dimension=0, tiled=True),
        lax.psum_scatter(grad_vals, "head", scatter_dimension=0, tiled=True),
    )
    grad_qweight = lax.psum(jnp.stack(weight_grads, axis=0), "ctx")
    grad_kweight = lax.psum(grad_kweight, ("ctx", "head"))
    return (
        jnp.concatenate(query_grads, axis=1),
        grad_keys,
        grad_values,
        grad_qweight,
        grad_kweight,
    )


def solution(mesh):
    placed = (
        P("ctx", "head"),
        P("ctx", None),
        P("ctx", None),
        P("ctx", "head"),
        P("ctx"),
        P(),
        P("head", None, None),
        P(),
    )
    return jax.shard_map(
        on_device,
        mesh=mesh,
        in_specs=placed,
        out_specs=(
            P("ctx", "head"),
            P(("ctx", "head"), None),
            P(("ctx", "head"), None),
            P("head", None, None),
            P(),
        ),
        check_vma=False,
    )
```

profile of v0, /device:TPU:1, one launch (start us, length us, event | category | flops | bytes accessed | tf_op | source)
XLA Modules:
  0.0 1215.2 jit_solution(13639607046449780209)
XLA Ops:
  7.2 1.5 fusion.97
  9.8 2.1 fusion.103
  14.9 74.7 %all-gather.4 = f32[64,1,256]{2,1,0:T(1,128)S(1)} all-gather(f32[1,1,256]{2,1,0:T(1,128)S(1)} %bitcast.226), channel_id=3, replica_groups=mesh['ctx'=64,'head'=8] {'ctx'}, dimensions={0}, use_global_device_ids=true | all-gather | bytes 66560 | tf_op jit(solution)/shard_map/all_gather | solution.py:9
  93.4 1.8 fusion.102
  95.2 1.8 fusion.104
  96.9 70.0 %all-gather.9.cloned.1.call-done = f32[16384,128]{1,0:T(8,128)} async-done(((f32[256,128]{1,0:T(8,128)}), f32[16384,128]{1,0:T(8,128)}) %all-gather.9.cloned.1.call-update) | async-done | bytes 8388624 | tf_op jit(solution)/shard_map/all_gather | solution.py:9
  166.9 106.3 %while.32 = (s32[]{:T(128)}, f32[256,128]{1,0:T(8,128)S(1)}, f32[256]{0:T(256)S(1)}, s32[]{:T(128)}, f32[64,256,128]{2,1,0:T(8,128)}, /*index=5*/f32[64,256]{1,0:T(8,128)}, s32[]{:T(128)}, s32[]{:T(128)}) while((s32[]{:T(128)}, f32[256,128]{1,0:T(8,128)S(1)}, f32[256]{0:T(256)S(1)}, s32[]{:T(128)}, f32[64,256,128]{2,1,0:T(8,128)}, ...), condition=%wide.region_15.16_spmd.clone, body=%wide.region_14.15_spmd.clone.sunk | while | flops 99076 | bytes 398459 | solution.py:21
  274.9 2.1 fusion.105
  279.6 1.6 fusion.14
  282.2 1.6 fusion.15
  285.0 64.7 %all-gather.5 = f32[64,1,256]{2,1,0:T(1,128)S(1)} all-gather(f32[1,1,256]{2,1,0:T(1,128)S(1)} %bitcast.225), channel_id=5, replica_groups=mesh['ctx'=64,'head'=8] {'ctx'}, dimensions={0}, use_global_device_ids=true | all-gather | bytes 66560 | tf_op jit(solution)/shard_map/all_gather | solution.py:9
  353.7 1.8 copy.214
  355.4 1.8 copy.215
  360.0 1.6 fusion.6
  363.9 1.5 fusion.44
  366.7 1.6 convolution_add_fusion.2
  368.2 1.4 fusion.4
  369.6 2.0 copy.209
  371.7 1.8 copy.213
  375.6 1.4 convolution_bitcast_fusion.2
  381.3 1.7 fusion.93
  384.1 1.6 fusion.7
  385.8 42.8 %all-gather.11.cloned.1.call-done = f32[16384,128]{1,0:T(8,128)} async-done(((f32[256,128]{1,0:T(8,128)}), f32[16384,128]{1,0:T(8,128)}) %all-gather.11.cloned.1.call-update) | async-done | bytes 8388624 | tf_op jit(solution)/shard_map/all_gather | solution.py:9
  428.5 7.7 rev.6
  436.2 106.4 %while.33 = (s32[]{:T(128)}, f32[256,128]{1,0:T(8,128)S(1)}, f32[256]{0:T(256)S(1)}, s32[]{:T(128)}, f32[64,256,128]{2,1,0:T(8,128)}, /*index=5*/f32[64,256]{1,0:T(8,128)}, s32[]{:T(128)}, s32[]{:T(128)}) while((s32[]{:T(128)}, f32[256,128]{1,0:T(8,128)S(1)}, f32[256]{0:T(256)S(1)}, s32[]{:T(128)}, f32[64,256,128]{2,1,0:T(8,128)}, ...), condition=%wide.region_33.34_spmd.clone, body=%wide.region_32.33_spmd.clone.sunk | while | flops 99076 | bytes 398459 | solution.py:21
  544.7 1.7 convolution_add_fusion.5
  549.7 135.7 %all-reduce.3.cloned.1.call-done = f32[2,128,128]{1,2,0:T(8,128)} async-done(((f32[2,128,128]{1,2,0:T(8,128)}), f32[2,128,128]{1,2,0:T(8,128)}) %all-reduce.3.cloned.1.call-update) | async-done | bytes 131088 | tf_op jit(solution)/shard_map/psum | solution.py:152
  685.3 1.7 copy.181
  687.0 449.9 %all-reduce.5.cloned.1.call-done = f32[128,128]{0,1:T(8,128)} async-done(((f32[128,128]{0,1:T(8,128)}), f32[128,128]{0,1:T(8,128)}) %all-reduce.5.cloned.1.call-update) | async-done | bytes 65552 | tf_op jit(solution)/shard_map/psum | solution.py:153
  1136.9 1.6 copy.182
  1138.4 29.6 %reduce-scatter.5.cloned.1.call-done = f32[64,128]{1,0:T(8,128)} async-done(((f32[512,128]{1,0:T(8,128)}), f32[64,128]{1,0:T(8,128)}) %reduce-scatter.5.cloned.1.call-update) | async-done | bytes 32784 | tf_op jit(solution)/shard_map/reduce_scatter | solution.py:150
  1168.1 40.3 %reduce-scatter.3.cloned.1.call-done = f32[64,128]{1,0:T(8,128)} async-done(((f32[512,128]{1,0:T(8,128)}), f32[64,128]{1,0:T(8,128)}) %reduce-scatter.3.cloned.1.call-update) | async-done | bytes 32784 | tf_op jit(solution)/shard_map/reduce_scatter | solution.py:149
  (489 shorter events, 246.6 us)
Async XLA Ops:
  7.2 2.6 copy-start
  7.2 84.9 %copy-start.12 = (f32[2,128,128]{2,1,0:T(8,128)S(1)}, f32[2,128,128]{2,1,0:T(8,128)}, u32[]{:S(2)}) copy-start(f32[2,128,128]{2,1,0:T(8,128)} %param.18) | copy-start | bytes 393220
  7.2 84.9 %copy-start.4 = (f32[512,256]{1,0:T(8,128)S(1)}, f32[512,256]{1,0:T(8,128)}, u32[]{:S(2)}) copy-start(f32[512,256]{1,0:T(8,128)} %param.12) | copy-start | bytes 1572868
  7.2 159.7 %all-gather.9.cloned.1.call-start = ((), (), s32[]{:S(2)}) async-start(), calls=%async_computation.6 | async-start | bytes 8519680 | tf_op jit(solution)/shard_map/all_gather | solution.py:9
  11.9 416.6 %all-gather.11.cloned.1.call-start = ((), (), s32[]{:S(2)}) async-start(), calls=%async_computation.7 | async-start | bytes 8519680 | tf_op jit(solution)/shard_map/all_gather | solution.py:9
  91.9 182.4 %copy-start.8 = (f32[4,128,128]{1,2,0:T(8,128)S(1)}, f32[4,128,128]{1,2,0:T(8,128)}, u32[]{:S(2)}) copy-start(f32[4,128,128]{1,2,0:T(8,128)} %copy.142) | copy-start | bytes 786436
  92.1 181.1 %copy-start.10 = (f32[128,128]{0,1:T(8,128)}, f32[128,128]{0,1:T(8,128)S(1)}, u32[]{:S(2)}) copy-start(f32[128,128]{0,1:T(8,128)S(1)} %fusion.88) | copy-start | bytes 196612
  273.3 77.0 %copy-start.11 = (f32[128,128]{0,1:T(8,128)S(1)}, f32[128,128]{0,1:T(8,128)}, u32[]{:S(2)}) copy-start(f32[128,128]{0,1:T(8,128)} %copy-done.10) | copy-start | bytes 196612
  277.0 408.4 %all-reduce.3.cloned.1.call-start = ((), (), s32[]{:S(2)}) async-start(), calls=%async_computation.4 | async-start | bytes 262144 | tf_op jit(solution)/shard_map/psum | solution.py:152
  285.0 75.0 %copy-start.15 = (f32[256]{0:T(256)}, f32[256]{0:T(256)S(1)}, u32[]{:S(2)}) copy-start(f32[256]{0:T(256)S(1)} %get-tuple-element.329) | copy-start | bytes 3076
  350.8 0.7 copy-start.6
  358.6 0.7 copy-start.7
  361.6 11.9 copy-start.3
  375.6 3.7 copy-start.1
  385.7 751.2 %all-reduce.5.cloned.1.call-start = ((), (), s32[]{:S(2)}) async-start(), calls=%async_computation.5 | async-start | bytes 131072 | tf_op jit(solution)/shard_map/psum | solution.py:153
  428.5 114.1 %copy-start.5 = (f32[512,256]{0,1:T(8,128)S(1)}, f32[512,256]{0,1:T(8,128)}, u32[]{:S(2)}) copy-start(f32[512,256]{0,1:T(8,128)} %copy.209) | copy-start | bytes 1572868
  428.5 114.9 %copy-start.9 = (f32[512,128]{1,0:T(8,128)S(1)}, f32[512,128]{1,0:T(8,128)}, u32[]{:S(2)}) copy-start(f32[512,128]{1,0:T(8,128)} %param.13) | copy-start | bytes 786436
  428.5 118.0 %copy-start.14 = (f32[128,128]{1,0:T(8,128)S(1)}, f32[128,128]{1,0:T(8,128)}, u32[]{:S(2)}) copy-start(f32[128,128]{1,0:T(8,128)} %param.19) | copy-start | bytes 196612
  436.2 111.6 %copy-start.2 = (f32[512,128]{0,1:T(8,128)S(1)}, f32[512,128]{0,1:T(8,128)}, u32[]{:S(2)}) copy-start(f32[512,128]{0,1:T(8,128)} %copy-done.1) | copy-start | bytes 786436
  436.2 111.6 %copy-start.13 = (f32[2,128,128]{2,1,0:T(8,128)S(1)}, f32[2,128,128]{2,1,0:T(8,128)}, u32[]{:S(2)}) copy-start(f32[2,128,128]{2,1,0:T(8,128)} %param.18) | copy-start | bytes 393220
  544.4 623.6 %reduce-scatter.5.cloned.1.call-start = ((), (), s32[]{:S(2)}) async-start(), calls=%async_computation.3 | async-start | bytes 294912 | tf_op jit(solution)/shard_map/reduce_scatter | solution.py:150
  546.4 661.9 %reduce-scatter.3.cloned.1.call-start = ((), (), s32[]{:S(2)}) async-start(), calls=%async_computation.2 | async-start | bytes 294912 | tf_op jit(solution)/shard_map/reduce_scatter | solution.py:149
Sparse Core Ops, SparseCore 0:
  12.0 154.8 all-gather.8
  277.1 151.3 all-gather.10
  431.9 253.3 all-reduce.2
  691.2 445.6 all-reduce.4
  1140.3 27.6 reduce-scatter.4
  1171.3 37.0 reduce-scatter.2
where the time goes:
time: 1220 us
  waiting for transfers between devices  768 us (63%)
  blocking collectives  139 us (11%)
  other arithmetic  133 us (11%)
  local copies, waits for them, and re-layouts  116 us (10%)
  matrix products  40.2 us (3%)
  between operations  14.6 us (1%)
    psum x1, waiting for transfers between devices, on_device(): grad_kweight = lax.psum(grad_kweight, ('ctx', 'head'))  450 us
    all_gather x2, blocking collectives, entering(): pieces = jax.tree.map(lambda part: lax.all_gather(part, axis), value)  139 us
    psum x1, waiting for transfers between devices, on_device(): grad_qweight = lax.psum(jnp.stack(weight_grads, axis=0), 'ctx')  136 us
    select_n x252, other arithmetic, turn(): jnp.where(position < mine, new, old)  121 us
    all_gather x2, waiting for transfers between devices, entering(): pieces = jax.tree.map(lambda part: lax.all_gather(part, axis), value)  113 us
    dynamic_slice x126, local copies, waits for them, and re-layouts, turn(): longer = join(total, jax.tree.map(lambda part: part[position], pieces))  89 us
    reduce_scatter x1, waiting for transfers between devices, on_device(): lax.psum_scatter(grad_key_part, 'head', scatter_dimension=0, tiled=True)  40.3 us
    dot_general x25, matrix products, product(): jnp.einsum(form, left, right, precision=lax.Precision.HIGHEST, preferred_...  29.7 us
  transfers between devices with their start and end apart: 6, of which 6 were waited for; matrix products, arithmetic and copies ran while one was open for 14% of the time, Pallas kernels for 0%

commit v1 on v0

v1 whole, which is shorter than its diff:
```python
import jax
import jax.numpy as jnp
from jax import lax
from jax.experimental import pallas as pl
from jax.experimental.pallas import tpu as pltpu
from jax.sharding import PartitionSpec as P

MESH = pl.DeviceIdType.MESH
F32 = jnp.float32
BF16 = jnp.bfloat16
NN = ((1,), (0,))
NT = ((1,), (1,))
TN = ((0,), (0,))
XN = 4
ZN = 16
HN = 8
GN = XN * HN
ROWS = 512
CH = 256
D = 128
NC = ROWS // CH
OWN = ROWS // HN
TR = 2 * D // GN
TM = TR + 2
TP = TR + 8
KW = D // GN
QX = 2 * D // XN
QZ = QX // ZN


def split(a):
    high = a.astype(BF16)
    return high, (a - high.astype(F32)).astype(BF16)


def dot(a, b, dims):
    return lax.dot_general(a, b, (dims, ((), ())), preferred_element_type=F32)


def mm3(a, b, dims):
    (ah, al), (bh, bl) = a, b
    return dot(ah, bh, dims) + (dot(ah, bl, dims) + dot(al, bh, dims))


def total(parts):
    acc = parts[0]
    for i in range(1, XN):
        acc = acc + parts[i]
    return acc


def features(inputs, weight):
    logits = jnp.dot(inputs, weight, precision=lax.Precision.HIGHEST, preferred_element_type=F32)
    upper = jnp.exp(logits - jnp.max(logits, axis=1, keepdims=True))
    lower = jnp.exp(jnp.min(logits, axis=1, keepdims=True) - logits)
    upper = upper * (1.0 / jnp.sum(upper, axis=1, keepdims=True))
    lower = lower * (1.0 / jnp.sum(lower, axis=1, keepdims=True))
    return upper, lower


def back(upper, lower, a, b):
    up = upper * (a - jnp.sum(upper * a, axis=1, keepdims=True))
    return up - lower * (b - jnp.sum(lower * b, axis=1, keepdims=True))


def column(row):
    return jnp.transpose(jnp.broadcast_to(row, (D, D)))


def kernel(
    q_ref, k_ref, v_ref, c_ref, ids_ref, sw_ref, qw_ref, kw_ref,
    gq_ref, gk_ref, gv_ref, gqw_ref, gkw_ref,
    kf, kh, kl, vh, vl, qf, qh, ql, sh, sl, intra, scaled, st, gnh, gnl, gnorm, c1, gkf, gval,
    sa, ra, ta, za, gas, ga, cb, rb, tb, zb, gbs, gb, ks, kr, qs, rq, tq, zq, gzs, gz, gx, ck, rc, tc, zc, gcs, gc,
    s_one, s_two, r_one, r_two,
):
    pos = lax.axis_index("ctx")
    h = lax.axis_index("head")
    z = pos // XN
    x = pos % XN
    me = h * XN + x

    def group_peer(i):
        t = (me + i) % GN
        return t, t % XN, t // XN

    def each_group(act):
        def step(i, carry):
            act(*group_peer(i))
            return carry
        lax.fori_loop(1, GN, step, 0)

    barrier = pltpu.get_barrier_semaphore()

    def greet(ctx, head):
        pl.semaphore_signal(barrier, inc=1, device_id=(ctx, head), device_id_type=MESH)

    za[...] = jnp.zeros_like(za)
    zb[...] = jnp.zeros_like(zb)
    each_group(lambda t, xp, hp: greet(z * XN + xp, hp))

    def greet_z(i, carry):
        greet(((z + i) % ZN) * XN + x, h)
        return carry
    lax.fori_loop(1, ZN, greet_z, 0)

    def start(src, dst, ssem, rsem, ctx, head):
        pltpu.make_async_remote_copy(
            src_ref=src, dst_ref=dst, send_sem=ssem, recv_sem=rsem,
            device_id=(ctx, head), device_id_type=MESH,
        ).start()

    def drain(ref, sem):
        pltpu.make_async_copy(ref, ref, sem).wait()

    def send_group(src_of, dst, index):
        each_group(lambda t, xp, hp: start(
            src_of(t, xp, hp), dst.at[me], s_one.at[index], r_one.at[index], z * XN + xp, hp))

    def recv_group(dst, index):
        drain(dst.at[pl.ds(0, GN - 1)], r_one.at[index])

    def sent_group(dst, index):
        drain(dst.at[pl.ds(0, GN - 1)], s_one.at[index])

    def send_x(src_of, dst, index):
        def step(i, carry):
            xp = (x + i) % XN
            start(src_of(xp), dst.at[x], s_one.at[index], r_one.at[index], z * XN + xp, h)
            return carry
        lax.fori_loop(1, XN, step, 0)

    def recv_x(dst, index):
        drain(dst.at[pl.ds(0, XN - 1)], r_one.at[index])

    def sent_x(dst, index):
        drain(dst.at[pl.ds(0, XN - 1)], s_one.at[index])

    def send_z(src_of, dst, index, low, high):
        def step(zp, carry):
            @pl.when(zp != z)
            def _():
                start(src_of(zp), dst.at[z], s_two.at[index, zp], r_two.at[index, z], zp * XN + x, h)
            return carry
        lax.fori_loop(low, high, step, 0)

    def wait_z(dst, sems, index, low, high):
        def step(zp, carry):
            @pl.when(zp != z)
            def _():
                drain(dst.at[zp], sems.at[index, zp])
            return carry
        lax.fori_loop(low, high, step, 0)

    upper, lower = features(k_ref[...], kw_ref[...])
    kf[:, :D] = upper
    kf[:, D:] = lower
    kh[...], kl[...] = split(kf[...])
    vh[:, :D], vl[:, :D] = split(v_ref[...])
    vh[:, D:] = jnp.ones((ROWS, D), BF16)
    vl[:, D:] = jnp.zeros((ROWS, D), BF16)
    tot = []
    for c in range(NC):
        r = pl.ds(c * CH, CH)
        st[c] = mm3((kh[r, :], kl[r, :]), (vh[r, :D], vl[r, :D]), TN)
        tot.append((jnp.sum(kf[r, :D], axis=0, keepdims=True), jnp.sum(kf[r, D:], axis=0, keepdims=True)))
    tot_all = jnp.concatenate([tot[0][0] + tot[1][0], tot[0][1] + tot[1][1]], axis=0)
    mine = st[0, pl.ds(h * (XN * TR), XN * TR), :] + st[1, pl.ds(h * (XN * TR), XN * TR), :]
    for i in range(XN):
        sa[i, :TR] = mine[TR * i:TR * i + TR]
        sa[i, TR:TM] = tot_all
    pl.semaphore_wait(barrier, GN - 1 + ZN - 1)
    send_x(lambda xp: sa.at[xp, pl.ds(0, TM)], ra.at[:, pl.ds(0, TM)], 0)
    ra[x] = sa[x]

    ids = ids_ref[...]
    onehot = (lax.broadcasted_iota(jnp.int32, (64, ROWS), 0) == ids).astype(F32).astype(BF16)
    diag = lax.broadcasted_iota(jnp.int32, (64, 64), 0) == lax.broadcasted_iota(jnp.int32, (64, 64), 1)
    wcol = jnp.sum(jnp.where(diag, sw_ref[...], 0.0), axis=1, keepdims=True)
    wtab = jnp.broadcast_to(wcol, (64, D))
    w1, rest = wtab.astype(BF16), wtab - wtab.astype(BF16).astype(F32)
    w2, w3 = split(rest)
    weight = dot(onehot, w1, TN) + dot(onehot, w2, TN) + dot(onehot, w3, TN)
    mask = lax.broadcasted_iota(jnp.int32, (CH, CH), 0) >= lax.broadcasted_iota(jnp.int32, (CH, CH), 1)

    def before(n):
        lanes = pl.ds(n * D, D)
        scaled[n] = c_ref[:, lanes] * weight
        upper, lower = features(q_ref[:, lanes], qw_ref[n])
        qf[n, :, :D] = upper
        qf[n, :, D:] = lower
        qh[n], ql[n] = split(qf[n])
        for c in range(NC):
            r = pl.ds(c * CH, CH)
            s = mm3((qh[n, r, :], ql[n, r, :]), (kh[r, :], kl[r, :]), NT)
            sh[n, r, :], sl[n, r, :] = split(jnp.where(mask, s, 0.0))
            intra[n, r, :] = mm3((sh[n, r, :], sl[n, r, :]), (vh[r, :], vl[r, :]), NN)

    recv_x(ra.at[:, pl.ds(0, TM)], 0)
    ta[...] = total(ra)
    send_z(lambda zp: ta.at[pl.ds(0, TM)], za.at[:, pl.ds(0, TM)], 0, z + 1, ZN)
    before(0)
    wait_z(za.at[:, pl.ds(0, TM)], r_two, 0, 0, z)
    pre = jnp.sum(za[...], axis=0)
    pre_tot = pre[TR:TM]
    for i in range(XN):
        gas[i] = pre[:TR]
        if i < XN - 1:
            pre = pre + ra[i]
            pre_tot = pre_tot + jnp.where(i < x, ra[i, TR:TM], 0.0)
    send_group(lambda t, xp, hp: gas.at[xp], ga, 1)
    ga[me] = gas[x]
    before(1)
    recv_group(ga, 1)

    p_now = ga[...].reshape(2 * D, D)
    tot_now = (pre_tot[0:1], pre_tot[1:2])
    states, totals = [], []
    for c in range(NC):
        states.append(split(p_now))
        totals.append(tot_now)
        if c < NC - 1:
            p_now = p_now + st[c]
            tot_now = (tot_now[0] + tot[c][0], tot_now[1] + tot[c][1])
    ct = [[0.0, 0.0] for _ in range(NC)]
    carried = []
    for c in range(NC):
        r = pl.ds(c * CH, CH)
        thi, tlo = split(jnp.concatenate([column(totals[c][0]), column(totals[c][1])], axis=0))
        full = (jnp.concatenate([states[c][0], thi], axis=1), jnp.concatenate([states[c][1], tlo], axis=1))
        acc = None
        for n in range(2):
            q = (qh[n, r, :], ql[n, r, :])
            nn = intra[n, r, :] + mm3(q, full, NN)
            inv = 1.0 / nn[:, D:]
            sc = scaled[n, r, :]
            gnum = sc * inv
            gno = -jnp.sum(sc * (nn[:, :D] * inv), axis=1, keepdims=True) * inv
            gnorm[n, r, :] = gno
            g = split(gnum)
            gnh[n, r, :], gnl[n, r, :] = g
            ct[c][0] = ct[c][0] + jnp.sum(gno * qf[n, r, :D], axis=0, keepdims=True)
            ct[c][1] = ct[c][1] + jnp.sum(gno * qf[n, r, D:], axis=0, keepdims=True)
            term = mm3(q, g, TN)
            acc = term if acc is None else acc + term
        carried.append(acc)
    c1[...] = carried[1]
    whole = carried[0] + carried[1]
    ct_all = jnp.concatenate([ct[0][0] + ct[1][0], ct[0][1] + ct[1][1]], axis=0)
    for t in range(GN):
        cb[t, :TR] = whole[TR * t:TR * t + TR]
        cb[t, TR:TM] = ct_all
    send_group(lambda t, xp, hp: cb.at[t, pl.ds(0, TM)], rb.at[:, pl.ds(0, TM)], 2)
    rb[me] = cb[me]

    def after(n):
        lanes = pl.ds(n * D, D)
        wpair = split(qw_ref[n])
        xs = split(q_ref[:, lanes])
        grads = []
        for c in range(NC):
            r = pl.ds(c * CH, CH)
            g = (gnh[n, r, :], gnl[n, r, :])
            gno = gnorm[n, r, :]
            gs = mm3(g, (vh[r, :D], vl[r, :D]), NT) + jnp.concatenate([gno, gno], axis=1)
            gs = split(jnp.where(mask, gs, 0.0))
            gfeat = mm3(gs, (kh[r, :], kl[r, :]), NN) + mm3(g, states[c], NT)
            a = gfeat[:, :D] + gno * totals[c][0]
            b = gfeat[:, D:] + gno * totals[c][1]
            gl = split(back(qf[n, r, :D], qf[n, r, D:], a, b))
            grads.append(gl)
            gq_ref[r, lanes] = mm3(gl, wpair, NT)
            gk = mm3(gs, (qh[n, r, :], ql[n, r, :]), TN)
            gv = mm3((sh[n, r, :], sl[n, r, :]), g, TN)
            if n == 0:
                gkf[r, :] = gk
                gval[r, :] = gv
            else:
                gkf[r, :] += gk
                gval[r, :] += gv
        gl = (jnp.concatenate([g[0] for g in grads], axis=0), jnp.concatenate([g[1] for g in grads], axis=0))
        gw = mm3(xs, gl, TN)
        parts = XN // 2
        for i in range(parts):
            qs[parts * n + i] = gw[QX * i:QX * i + QX]

    after(0)
    recv_group(rb.at[:, pl.ds(0, TM)], 2)
    by_x = []
    for i in range(XN):
        s = rb[i]
        for hp in range(1, HN):
            s = s + rb[hp * XN + i]
        by_x.append(s)
    tb[...] = total(by_x)
    send_z(lambda zp: tb.at[pl.ds(0, TM)], zb.at[:, pl.ds(0, TM)], 1, 0, z)
    after(1)
    send_x(lambda xp: qs.at[xp], rq, 3)
    rq[x] = qs[x]

    wait_z(zb.at[:, pl.ds(0, TM)], r_two, 1, z + 1, ZN)
    suf = jnp.sum(zb[...], axis=0)
    suf_tot = suf[TR:TM]
    for i in reversed(range(XN)):
        gbs[i] = suf[:TR]
        if i > 0:
            suf = suf + by_x[i]
            suf_tot = suf_tot + jnp.where(i > x, by_x[i][TR:TM], 0.0)
    send_group(lambda t, xp, hp: gbs.at[xp], gb, 4)
    gb[me] = gbs[x]

    r = pl.ds(0, CH)
    cpair = split(c1[...])
    gkf[r, :] += mm3((vh[r, :D], vl[r, :D]), cpair, NT) + jnp.concatenate([ct[1][0], ct[1][1]], axis=1)
    gval[r, :] += mm3((kh[r, :], kl[r, :]), cpair, NN)
    gl = back(kf[:, :D], kf[:, D:], gkf[:, :D], gkf[:, D:])
    for i in range(HN):
        ks[i, :, :D] = gl[OWN * i:OWN * i + OWN]
        ks[i, :, D:] = gval[OWN * i:OWN * i + OWN, :]

    def send_key(i, carry):
        hp = (h + i) % HN
        start(ks.at[hp], kr.at[h], s_one.at[5], r_one.at[5], pos, hp)
        return carry
    lax.fori_loop(1, HN, send_key, 0)
    kr[h] = ks[h]

    recv_x(rq, 3)
    tsum = total(rq)
    for i in range(ZN):
        tq[i] = tsum[QZ * i:QZ * i + QZ]
    send_z(lambda zp: tq.at[zp], zq, 2, 0, ZN)
    zq[z] = tq[z]

    recv_group(gb, 4)
    later = split(gb[...].reshape(2 * D, D))
    own = pl.ds(h * OWN, OWN)
    v64 = (vh[own, :D], vl[own, :D])
    gfeat = mm3(v64, later, NT)
    gval64 = mm3((kh[own, :], kl[own, :]), later, NN)
    gl = back(kf[own, :D], kf[own, D:], gfeat[:, :D] + suf_tot[0:1], gfeat[:, D:] + suf_tot[1:2])
    drain(kr.at[pl.ds(0, HN - 1)], r_one.at[5])
    got = kr[0]
    for i in range(1, HN):
        got = got + kr[i]
    glp = split(gl + got[:, :D])
    gkw = mm3(split(k_ref[own, :]), glp, TN)
    for i in range(GN):
        ck[i] = gkw[KW * i:KW * i + KW]
    send_group(lambda t, xp, hp: ck.at[t], rc, 6)
    rc[me] = ck[me]
    gk_ref[...] = mm3(glp, split(kw_ref[...]), NT)
    gv_ref[...] = gval64 + got[:, D:]

    wait_z(zq, r_two, 2, 0, ZN)
    gzs[...] = jnp.sum(zq[...], axis=0)
    send_z(lambda zp: gzs, gz, 3, 0, ZN)
    gz[z] = gzs[...]

    recv_group(rc, 6)
    tc[...] = jnp.sum(rc[...], axis=0)
    send_z(lambda zp: tc, zc, 4, 0, ZN)
    zc[z] = tc[...]

    wait_z(gz, r_two, 3, 0, ZN)
    send_x(lambda xp: gz, gx, 7)
    gx[x] = gz[...]

    wait_z(zc, r_two, 4, 0, ZN)
    gcs[...] = jnp.sum(zc[...], axis=0)
    send_group(lambda t, xp, hp: gcs, gc, 8)
    gc[me] = gcs[...]

    recv_x(gx, 7)
    for i in range(XN):
        for j in range(ZN):
            row = QX * i + QZ * j
            gqw_ref[row // D, row % D:row % D + QZ, :] = gx[i, j]
    recv_group(gc, 8)
    for i in range(GN):
        gkw_ref[KW * i:KW * i + KW, :] = gc[i]

    sent_x(ra.at[:, pl.ds(0, TM)], 0)
    sent_group(ga, 1)
    sent_group(rb.at[:, pl.ds(0, TM)], 2)
    sent_x(rq, 3)
    sent_group(gb, 4)
    drain(kr.at[pl.ds(0, HN - 1)], s_one.at[5])
    sent_group(rc, 6)
    sent_x(gx, 7)
    sent_group(gc, 8)
    wait_z(za.at[:, pl.ds(0, TM)], s_two, 0, z + 1, ZN)
    wait_z(zb.at[:, pl.ds(0, TM)], s_two, 1, 0, z)
    wait_z(zq, s_two, 2, 0, ZN)
    wait_z(gz, s_two, 3, 0, ZN)
    wait_z(zc, s_two, 4, 0, ZN)


def on_device(queries, keys, values, cotangent, source_ids, source_weights, q_feature, k_feature):
    def vm(*shape, dtype=F32):
        return pltpu.VMEM(shape, dtype)

    b = dict(dtype=BF16)
    vmem = pl.BlockSpec(memory_space=pltpu.VMEM)
    return pl.pallas_call(
        kernel,
        out_shape=(
            jax.ShapeDtypeStruct((ROWS, 2 * D), F32),
            jax.ShapeDtypeStruct((OWN, D), F32),
            jax.ShapeDtypeStruct((OWN, D), F32),
            jax.ShapeDtypeStruct((2, D, D), F32),
            jax.ShapeDtypeStruct((D, D), F32),
        ),
        in_specs=[vmem] * 8,
        out_specs=[vmem] * 5,
        scratch_shapes=[
            vm(ROWS, 2 * D), vm(ROWS, 2 * D, **b), vm(ROWS, 2 * D, **b),
            vm(ROWS, 2 * D, **b), vm(ROWS, 2 * D, **b),
            vm(2, ROWS, 2 * D), vm(2, ROWS, 2 * D, **b), vm(2, ROWS, 2 * D, **b),
            vm(2, ROWS, CH, **b), vm(2, ROWS, CH, **b),
            vm(2, ROWS, 2 * D), vm(2, ROWS, D), vm(NC, 2 * D, D),
            vm(2, ROWS, D, **b), vm(2, ROWS, D, **b), vm(2, ROWS, D),
            vm(2 * D, D), vm(ROWS, 2 * D), vm(ROWS, D),
            vm(XN, TP, D), vm(XN, TP, D), vm(TP, D), vm(ZN, TP, D), vm(XN, TR, D), vm(GN, TR, D),
            vm(GN, TP, D), vm(GN, TP, D), vm(TP, D), vm(ZN, TP, D), vm(XN, TR, D), vm(GN, TR, D),
            vm(HN, OWN, 2 * D), vm(HN, OWN, 2 * D),
            vm(XN, QX, D), vm(XN, QX, D), vm(ZN, QZ, D), vm(ZN, QZ, D),
            vm(QZ, D), vm(ZN, QZ, D), vm(XN, ZN, QZ, D),
            vm(GN, KW, D), vm(GN, KW, D), vm(KW, D), vm(ZN, KW, D), vm(KW, D), vm(GN, KW, D),
            pltpu.SemaphoreType.DMA((9,)),
            pltpu.SemaphoreType.DMA((5, ZN)),
            pltpu.SemaphoreType.DMA((9,)),
            pltpu.SemaphoreType.DMA((5, ZN)),
        ],
        compiler_params=pltpu.CompilerParams(
            collective_id=0, has_side_effects=True, vmem_limit_bytes=48 * 1024 * 1024
        ),
        cost_estimate=pl.CostEstimate(flops=3_000_000_000, bytes_accessed=2_500_000, transcendentals=400_000),
    )(queries, keys, values, cotangent, source_ids.reshape(1, ROWS), source_weights.reshape(1, -1), q_feature, k_feature)


def solution(mesh):
    placed = (
        P("ctx", "head"),
        P("ctx", None),
        P("ctx", None),
        P("ctx", "head"),
        P("ctx"),
        P(),
        P("head", None, None),
        P(),
    )
    return jax.shard_map(
        on_device,
        mesh=mesh,
        in_specs=placed,
        out_specs=(
            P("ctx", "head"),
            P(("ctx", "head"), None),
            P(("ctx", "head"), None),
            P("head", None, None),
            P(),
        ),
        check_vma=False,
    )
```

time: 1220 us -> 86.4 us (0.07)
  waiting for transfers between devices: 768 us -> 0 us
  blocking collectives: 139 us -> 0 us
  other arithmetic: 133 us -> 0 us
  local copies, waits for them, and re-layouts: 116 us -> 9.7 us
  Pallas kernels: 0 us -> 75.7 us
  matrix products: 40.2 us -> 0 us
  between operations: 14.6 us -> 0.67 us
    psum x2 -> x0, waiting for transfers between devices: 586 us -> none  [the longest x1 450 us: on_device(): grad_kweight = lax.psum(grad_kweight, ('ctx', 'head'))]
    all_gather x2 -> x0, blocking collectives: 139 us -> none  [entering(): pieces = jax.tree.map(lambda part: lax.all_gather(part, axis), value)]
    select_n x252 -> x0, other arithmetic: 121 us -> none  [turn(): jnp.where(position < mine, new, old)]
    all_gather x2 -> x0, waiting for transfers between devices: 113 us -> none  [entering(): pieces = jax.tree.map(lambda part: lax.all_gather(part, axis), value)]
    dynamic_slice x126 -> x0, local copies, waits for them, and re-layouts: 89 us -> none  [turn(): longer = join(total, jax.tree.map(lambda part: part[position], pieces))]
    pallas_call x0 -> x1, Pallas kernels: none -> 75.7 us  [on_device(): pl.pallas_call(kernel, out_shape=(jax.ShapeDtypeStruct((ROWS, 2 * D), F32...]
    reduce_scatter x2 -> x0, waiting for transfers between devices: 69.9 us -> none  [the longest x1 40.3 us: on_device(): lax.psum_scatter(grad_key_part, 'head', scatter_dimension=0, tiled=True)]
    dot_general x36 -> x0, matrix products: 40.2 us -> none  [the longest x25 29.7 us: product(): jnp.einsum(form, left, right, precision=lax.Precision.HIGHEST, preferred_...]
  transfers between devices with their start and end apart: 6 -> 0, of which waited for: 6 -> 0; matrix products, arithmetic and copies ran while one was open for 14% -> 0% of each run, Pallas kernels for 0% -> 0%
where the time goes in v1:
time: 86.4 us; the launch traced here: 86.1 us
  Pallas kernels  75.7 us (88%)
  local copies, waits for them, and re-layouts  9.7 us (11%)
    pallas_call x1, Pallas kernels, on_device(): pl.pallas_call(kernel, out_shape=(jax.ShapeDtypeStruct((ROWS, 2 * D), F32...  75.7 us
    unnamed x21, local copies, waits for them, and re-layouts  9.7 us

profile of v1, /device:TPU:1, one launch (start us, length us, event | category | flops | bytes accessed | tf_op | source)
XLA Modules:
  0.0 86.1 jit_solution(830001364795838663)
XLA Ops:
  0.6 0.0 copy-start.6
  0.6 0.0 copy-start.7
  0.7 0.7 copy-done.6
  1.3 0.0 copy-done.7
  1.3 0.0 copy-start
  1.3 1.0 %copy-done = f32[512,256]{1,0:T(8,128)S(1)} copy-done((f32[512,256]{1,0:T(8,128)S(1)}, f32[512,256]{1,0:T(8,128)}, u32[]{:S(2)}) %copy-start) | copy-done | bytes 524312
  2.4 0.0 copy-start.1
  2.4 1.0 %copy-done.1 = f32[512,256]{1,0:T(8,128)S(1)} copy-done((f32[512,256]{1,0:T(8,128)S(1)}, f32[512,256]{1,0:T(8,128)}, u32[]{:S(2)}) %copy-start.1) | copy-done | bytes 524312
  3.4 0.0 copy-start.2
  3.4 0.9 %copy-done.2 = f32[512,128]{1,0:T(8,128)S(1)} copy-done((f32[512,128]{1,0:T(8,128)S(1)}, f32[512,128]{1,0:T(8,128)}, u32[]{:S(2)}) %copy-start.2) | copy-done | bytes 262168
  4.4 0.0 copy-start.3
  4.4 0.9 %copy-done.3 = f32[512,128]{1,0:T(8,128)S(1)} copy-done((f32[512,128]{1,0:T(8,128)S(1)}, f32[512,128]{1,0:T(8,128)}, u32[]{:S(2)}) %copy-start.3) | copy-done | bytes 262168
  5.3 0.0 copy-start.4
  5.3 0.9 %copy-done.4 = f32[2,128,128]{2,1,0:T(8,128)S(1)} copy-done((f32[2,128,128]{2,1,0:T(8,128)S(1)}, f32[2,128,128]{2,1,0:T(8,128)}, u32[]{:S(2)}) %copy-start.4) | copy-done | bytes 131096
  6.2 0.0 copy-start.5
  6.2 0.8 copy-done.5
  7.0 75.7 %shard_map.119 = (f32[512,256]{1,0:T(8,128)S(1)}, f32[64,128]{1,0:T(8,128)S(1)}, f32[64,128]{1,0:T(8,128)S(1)}, f32[2,128,128]{2,1,0:T(8,128)S(1)}, f32[128,128]{1,0:T(8,128)S(1)}) custom-call(f32[512,256]{1,0:T(8,128)S(1)} %copy-done, f32[512,128]{1,0:T(8,128)S(1)} %copy-done.2, f32[512,128]{1,0:T(8,128)S(1)} %copy-done.3, f32[512,256]{1,0:T(8,128)S(1)} %copy-done.1, ...), custom_call_target="tpu_custom_call" | custom-call | flops 3000000000 | bytes 2500000 | tf_op jit(solution)/shard_map/pallas_call | solution.py:405
  82.8 0.8 copy.18
  83.6 0.6 copy.19
  84.2 0.6 copy.20
  84.8 0.7 copy.21
  85.5 0.6 copy.22
Async XLA Ops:
  0.6 0.7 copy-start.6
  0.6 0.7 copy-start.7
  1.3 1.0 %copy-start = (f32[512,256]{1,0:T(8,128)S(1)}, f32[512,256]{1,0:T(8,128)}, u32[]{:S(2)}) copy-start(f32[512,256]{1,0:T(8,128)} %q_ref.1) | copy-start | bytes 1572868
  2.4 1.0 %copy-start.1 = (f32[512,256]{1,0:T(8,128)S(1)}, f32[512,256]{1,0:T(8,128)}, u32[]{:S(2)}) copy-start(f32[512,256]{1,0:T(8,128)} %c_ref.1) | copy-start | bytes 1572868
  3.4 0.9 %copy-start.2 = (f32[512,128]{1,0:T(8,128)S(1)}, f32[512,128]{1,0:T(8,128)}, u32[]{:S(2)}) copy-start(f32[512,128]{1,0:T(8,128)} %k_ref.1) | copy-start | bytes 786436
  4.4 0.9 %copy-start.3 = (f32[512,128]{1,0:T(8,128)S(1)}, f32[512,128]{1,0:T(8,128)}, u32[]{:S(2)}) copy-start(f32[512,128]{1,0:T(8,128)} %v_ref.1) | copy-start | bytes 786436
  5.3 0.9 %copy-start.4 = (f32[2,128,128]{2,1,0:T(8,128)S(1)}, f32[2,128,128]{2,1,0:T(8,128)}, u32[]{:S(2)}) copy-start(f32[2,128,128]{2,1,0:T(8,128)} %qw_ref.1) | copy-start | bytes 393220
  6.2 0.8 copy-start.5

commit v2 on v1

--- a/solution.py
+++ b/solution.py
@@ -67,11 +67,18 @@
     return jnp.transpose(jnp.broadcast_to(row, (D, D)))
 
 
+def swing(i, n):
+    return (n // 2 + ((i + 1) // 2) * (1 - 2 * (i % 2))) % n
+
+
 def kernel(
-    q_ref, k_ref, v_ref, c_ref, ids_ref, sw_ref, qw_ref, kw_ref,
-    gq_ref, gk_ref, gv_ref, gqw_ref, gkw_ref,
+    q_in, k_in, v_in, c_in, ids_in, sw_in, qw_in, kw_in,
+    gq_out, gk_out, gv_out, gqw_out, gkw_out,
+    gq_ref, gk_ref, gv_ref, gqw_ref, gkw_ref, o_sem,
+    q_ref, k_ref, v_ref, c_ref, ids_ref, sw_ref, qw_ref, kw_ref, i_sem,
     kf, kh, kl, vh, vl, qf, qh, ql, sh, sl, intra, scaled, st, gnh, gnl, gnorm, c1, gkf, gval,
     sa, ra, ta, za, gas, ga, cb, rb, tb, zb, gbs, gb, ks, kr, qs, rq, tq, zq, gzs, gz, gx, ck, rc, tc, zc, gcs, gc,
+    qth, qtl, kth, ktl, iks, ikr, gint,
     s_one, s_two, r_one, r_two,
 ):
     pos = lax.axis_index("ctx")
@@ -80,29 +87,45 @@
     x = pos % XN
     me = h * XN + x
 
-    def group_peer(i):
-        t = (me + i) % GN
-        return t, t % XN, t // XN
-
     def each_group(act):
         def step(i, carry):
-            act(*group_peer(i))
+            xp = (x + swing(i // HN, XN)) % XN
+            yp = (h // 2 + swing(i // 2 % (HN // 2), HN // 2)) % (HN // 2)
+            hp = yp * 2 + (h + i + 1) % 2
+            act(hp * XN + xp, xp, hp)
             return carry
-        lax.fori_loop(1, GN, step, 0)
+        lax.fori_loop(0, GN - 1, step, 0)
+
+    def each_z(act):
+        def step(i, carry):
+            act((z + swing(i, ZN)) % ZN)
+            return carry
+        lax.fori_loop(0, ZN - 1, step, 0)
 
     barrier = pltpu.get_barrier_semaphore()
 
     def greet(ctx, head):
         pl.semaphore_signal(barrier, inc=1, device_id=(ctx, head), device_id_type=MESH)
 
+    loads = [
+        pltpu.make_async_copy(src, dst, i_sem.at[i])
+        for i, (src, dst) in enumerate([
+            (k_in, k_ref), (kw_in, kw_ref), (v_in, v_ref), (q_in, q_ref),
+            (qw_in, qw_ref), (c_in, c_ref), (ids_in, ids_ref), (sw_in, sw_ref),
+        ])
+    ]
+    for load in loads:
+        load.start()
+    stores = [
+        pltpu.make_async_copy(src, dst, o_sem.at[i])
+        for i, (src, dst) in enumerate([
+            (gq_ref, gq_out), (gk_ref, gk_out), (gv_ref, gv_out), (gqw_ref, gqw_out), (gkw_ref, gkw_out),
+        ])
+    ]
     za[...] = jnp.zeros_like(za)
     zb[...] = jnp.zeros_like(zb)
+    each_z(lambda zp: greet(zp * XN + x, h))
     each_group(lambda t, xp, hp: greet(z * XN + xp, hp))
-
-    def greet_z(i, carry):
-        greet(((z + i) % ZN) * XN + x, h)
-        return carry
-    lax.fori_loop(1, ZN, greet_z, 0)
 
     def start(src, dst, ssem, rsem, ctx, head):
         pltpu.make_async_remote_copy(
@@ -125,10 +148,10 @@
 
     def send_x(src_of, dst, index):
         def step(i, carry):
-            xp = (x + i) % XN
+            xp = (x + swing(i, XN)) % XN
             start(src_of(xp), dst.at[x], s_one.at[index], r_one.at[index], z * XN + xp, h)
             return carry
-        lax.fori_loop(1, XN, step, 0)
+        lax.fori_loop(0, XN - 1, step, 0)
 
     def recv_x(dst, index):
         drain(dst.at[pl.ds(0, XN - 1)], r_one.at[index])
@@ -137,12 +160,11 @@
         drain(dst.at[pl.ds(0, XN - 1)], s_one.at[index])
 
     def send_z(src_of, dst, index, low, high):
-        def step(zp, carry):
-            @pl.when(zp != z)
+        def act(zp):
+            @pl.when((zp >= low) & (zp < high))
             def _():
                 start(src_of(zp), dst.at[z], s_two.at[index, zp], r_two.at[index, z], zp * XN + x, h)
-            return carry
-        lax.fori_loop(low, high, step, 0)
+        each_z(act)
 
     def wait_z(dst, sems, index, low, high):
         def step(zp, carry):
@@ -152,10 +174,13 @@
             return carry
         lax.fori_loop(low, high, step, 0)
 
+    loads[0].wait()
+    loads[1].wait()
     upper, lower = features(k_ref[...], kw_ref[...])
     kf[:, :D] = upper
     kf[:, D:] = lower
     kh[...], kl[...] = split(kf[...])
+    loads[2].wait()
     vh[:, :D], vl[:, :D] = split(v_ref[...])
     vh[:, D:] = jnp.ones((ROWS, D), BF16)
     vl[:, D:] = jnp.zeros((ROWS, D), BF16)
@@ -173,6 +198,10 @@
     send_x(lambda xp: sa.at[xp, pl.ds(0, TM)], ra.at[:, pl.ds(0, TM)], 0)
     ra[x] = sa[x]
 
+    for load in loads[3:]:
+        load.wait()
+    kth[...], ktl[...] = split(jnp.transpose(k_ref[...]))
+
     ids = ids_ref[...]
     onehot = (lax.broadcasted_iota(jnp.int32, (64, ROWS), 0) == ids).astype(F32).astype(BF16)
     diag = lax.broadcasted_iota(jnp.int32, (64, 64), 0) == lax.broadcasted_iota(jnp.int32, (64, 64), 1)
@@ -190,6 +219,7 @@
         qf[n, :, :D] = upper
         qf[n, :, D:] = lower
         qh[n], ql[n] = split(qf[n])
+        qth[n], qtl[n] = split(jnp.transpose(qf[n]))
         for c in range(NC):
             r = pl.ds(c * CH, CH)
             s = mm3((qh[n, r, :], ql[n, r, :]), (kh[r, :], kl[r, :]), NT)
@@ -241,7 +271,7 @@
             gnh[n, r, :], gnl[n, r, :] = g
             ct[c][0] = ct[c][0] + jnp.sum(gno * qf[n, r, :D], axis=0, keepdims=True)
             ct[c][1] = ct[c][1] + jnp.sum(gno * qf[n, r, D:], axis=0, keepdims=True)
-            term = mm3(q, g, TN)
+            term = mm3((qth[n, :, r], qtl[n, :, r]), g, NN)
             acc = term if acc is None else acc + term
         carried.append(acc)
     c1[...] = carried[1]
@@ -285,6 +315,8 @@
             qs[parts * n + i] = gw[QX * i:QX * i + QX]
 
     after(0)
+    after(1)
+    stores[0].start()
     recv_group(rb.at[:, pl.ds(0, TM)], 2)
     by_x = []
     for i in range(XN):
@@ -294,7 +326,28 @@
         by_x.append(s)
     tb[...] = total(by_x)
     send_z(lambda zp: tb.at[pl.ds(0, TM)], zb.at[:, pl.ds(0, TM)], 1, 0, z)
-    after(1)
+
+    r = pl.ds(0, CH)
+    cpair = split(c1[...])
+    gkf[r, :] += mm3((vh[r, :D], vl[r, :D]), cpair, NT) + jnp.concatenate([ct[1][0], ct[1][1]], axis=1)
+    gval[r, :] += mm3((kh[r, :], kl[r, :]), cpair, NN)
+    gl = back(kf[:, :D], kf[:, D:], gkf[:, :D], gkf[:, D:])
+    for i in range(HN):
+        ks[i, :, :D] = gl[OWN * i:OWN * i + OWN]
+        ks[i, :, D:] = gval[OWN * i:OWN * i + OWN, :]
+
+    def send_key(i, carry):
+        hp = (h + i) % HN
+        start(ks.at[hp], kr.at[h], s_one.at[5], r_one.at[5], pos, hp)
+        return carry
+    lax.fori_loop(1, HN, send_key, 0)
+    kr[h] = ks[h]
+    kpair = (kth[...], ktl[...])
+    gkw = mm3(kpair, split(gl), NN)
+    for i in range(GN):
+        iks[i] = gkw[KW * i:KW * i + KW]
+    send_group(lambda t, xp, hp: iks.at[t], ikr, 9)
+    ikr[me] = iks[me]
     send_x(lambda xp: qs.at[xp], rq, 3)
     rq[x] = qs[x]
 
@@ -309,76 +362,66 @@
     send_group(lambda t, xp, hp: gbs.at[xp], gb, 4)
     gb[me] = gbs[x]
 
-    r = pl.ds(0, CH)
-    cpair = split(c1[...])
-    gkf[r, :] += mm3((vh[r, :D], vl[r, :D]), cpair, NT) + jnp.concatenate([ct[1][0], ct[1][1]], axis=1)
-    gval[r, :] += mm3((kh[r, :], kl[r, :]), cpair, NN)
-    gl = back(kf[:, :D], kf[:, D:], gkf[:, :D], gkf[:, D:])
-    for i in range(HN):
-        ks[i, :, :D] = gl[OWN * i:OWN * i + OWN]
-        ks[i, :, D:] = gval[OWN * i:OWN * i + OWN, :]
-
-    def send_key(i, carry):
-        hp = (h + i) % HN
-        start(ks.at[hp], kr.at[h], s_one.at[5], r_one.at[5], pos, hp)
-        return carry
-    lax.fori_loop(1, HN, send_key, 0)
-    kr[h] = ks[h]
-
     recv_x(rq, 3)
     tsum = total(rq)
     for i in range(ZN):
         tq[i] = tsum[QZ * i:QZ * i + QZ]
     send_z(lambda zp: tq.at[zp], zq, 2, 0, ZN)
     zq[z] = tq[z]
+    recv_group(ikr, 9)
+    early = jnp.sum(ikr[...], axis=0)
 
     recv_group(gb, 4)
     later = split(gb[...].reshape(2 * D, D))
+    gfeat = mm3((vh[:, :D], vl[:, :D]), later, NT)
+    gl = back(kf[:, :D], kf[:, D:], gfeat[:, :D] + suf_tot[0:1], gfeat[:, D:] + suf_tot[1:2])
+    gkw = mm3(kpair, split(gl), NN)
+    for i in range(GN):
+        ck[i] = gkw[KW * i:KW * i + KW]
+    send_x(lambda xp: ck.at[h * XN + xp], rc, 6)
+    rc[x] = ck[me]
+    gint[...] = gl
+
     own = pl.ds(h * OWN, OWN)
-    v64 = (vh[own, :D], vl[own, :D])
-    gfeat = mm3(v64, later, NT)
-    gval64 = mm3((kh[own, :], kl[own, :]), later, NN)
-    gl = back(kf[own, :D], kf[own, D:], gfeat[:, :D] + suf_tot[0:1], gfeat[:, D:] + suf_tot[1:2])
     drain(kr.at[pl.ds(0, HN - 1)], r_one.at[5])
     got = kr[0]
     for i in range(1, HN):
         got = got + kr[i]
-    glp = split(gl + got[:, :D])
-    gkw = mm3(split(k_ref[own, :]), glp, TN)
-    for i in range(GN):
-        ck[i] = gkw[KW * i:KW * i + KW]
-    send_group(lambda t, xp, hp: ck.at[t], rc, 6)
-    rc[me] = ck[me]
-    gk_ref[...] = mm3(glp, split(kw_ref[...]), NT)
-    gv_ref[...] = gval64 + got[:, D:]
+    gk_ref[...] = mm3(split(gint[own, :] + got[:, :D]), split(kw_ref[...]), NT)
+    gv_ref[...] = mm3((kh[own, :], kl[own, :]), later, NN) + got[:, D:]
+
+    stores[1].start()
+    stores[2].start()
+
+    recv_x(rc, 6)
+    tc[...] = total(rc) + early
+    send_z(lambda zp: tc, zc, 4, 0, ZN)
+    zc[z] = tc[...]
 
     wait_z(zq, r_two, 2, 0, ZN)
     gzs[...] = jnp.sum(zq[...], axis=0)
     send_z(lambda zp: gzs, gz, 3, 0, ZN)
     gz[z] = gzs[...]
 
-    recv_group(rc, 6)
-    tc[...] = jnp.sum(rc[...], axis=0)
-    send_z(lambda zp: tc, zc, 4, 0, ZN)
-    zc[z] = tc[...]
-
-    wait_z(gz, r_two, 3, 0, ZN)
-    send_x(lambda xp: gz, gx, 7)
-    gx[x] = gz[...]
-
     wait_z(zc, r_two, 4, 0, ZN)
     gcs[...] = jnp.sum(zc[...], axis=0)
     send_group(lambda t, xp, hp: gcs, gc, 8)
     gc[me] = gcs[...]
+
+    wait_z(gz, r_two, 3, 0, ZN)
+    send_x(lambda xp: gz, gx, 7)
+    gx[x] = gz[...]
 
     recv_x(gx, 7)
     for i in range(XN):
         for j in range(ZN):
             row = QX * i + QZ * j
             gqw_ref[row // D, row % D:row % D + QZ, :] = gx[i, j]
+    stores[3].start()
     recv_group(gc, 8)
     for i in range(GN):
         gkw_ref[KW * i:KW * i + KW, :] = gc[i]
+    stores[4].start()
 
     sent_x(ra.at[:, pl.ds(0, TM)], 0)
     sent_group(ga, 1)
@@ -386,7 +429,8 @@
     sent_x(rq, 3)
     sent_group(gb, 4)
     drain(kr.at[pl.ds(0, HN - 1)], s_one.at[5])
-    sent_group(rc, 6)
+    sent_x(rc, 6)
+    sent_group(ikr, 9)
     sent_x(gx, 7)
     sent_group(gc, 8)
     wait_z(za.at[:, pl.ds(0, TM)], s_two, 0, z + 1, ZN)
@@ -394,6 +438,17 @@
     wait_z(zq, s_two, 2, 0, ZN)
     wait_z(gz, s_two, 3, 0, ZN)
     wait_z(zc, s_two, 4, 0, ZN)
+    for copy in stores:
+        copy.wait()
+
+
+def store(*refs):
+    sems = refs[10]
+    copies = [pltpu.make_async_copy(refs[i], refs[5 + i], sems.at[i]) for i in range(5)]
+    for copy in copies:
+        copy.start()
+    for copy in copies:
+        copy.wait()
 
 
 def on_device(queries, keys, values, cotangent, source_ids, source_weights, q_feature, k_feature):
@@ -401,8 +456,7 @@
         return pltpu.VMEM(shape, dtype)
 
     b = dict(dtype=BF16)
-    vmem = pl.BlockSpec(memory_space=pltpu.VMEM)
-    return pl.pallas_call(
+    results = pl.pallas_call(
         kernel,
         out_shape=(
             jax.ShapeDtypeStruct((ROWS, 2 * D), F32),
@@ -411,9 +465,12 @@
             jax.ShapeDtypeStruct((2, D, D), F32),
             jax.ShapeDtypeStruct((D, D), F32),
         ),
-        in_specs=[vmem] * 8,
-        out_specs=[vmem] * 5,
+        in_specs=[pl.BlockSpec(memory_space=pl.ANY)] * 8,
+        out_specs=[pl.BlockSpec(memory_space=pl.ANY)] * 5,
         scratch_shapes=[
+            vm(ROWS, 2 * D), vm(OWN, D), vm(OWN, D), vm(2, D, D), vm(D, D), pltpu.SemaphoreType.DMA((5,)),
+            vm(ROWS, 2 * D), vm(ROWS, D), vm(ROWS, D), vm(ROWS, 2 * D), vm(1, ROWS, dtype=jnp.int32), vm(1, 64),
+            vm(2, D, D), vm(D, D), pltpu.SemaphoreType.DMA((8,)),
             vm(ROWS, 2 * D), vm(ROWS, 2 * D, **b), vm(ROWS, 2 * D, **b),
             vm(ROWS, 2 * D, **b), vm(ROWS, 2 * D, **b),
             vm(2, ROWS, 2 * D), vm(2, ROWS, 2 * D, **b), vm(2, ROWS, 2 * D, **b),
@@ -426,17 +483,26 @@
             vm(HN, OWN, 2 * D), vm(HN, OWN, 2 * D),
             vm(XN, QX, D), vm(XN, QX, D), vm(ZN, QZ, D), vm(ZN, QZ, D),
             vm(QZ, D), vm(ZN, QZ, D), vm(XN, ZN, QZ, D),
-            vm(GN, KW, D), vm(GN, KW, D), vm(KW, D), vm(ZN, KW, D), vm(KW, D), vm(GN, KW, D),
-            pltpu.SemaphoreType.DMA((9,)),
+            vm(GN, KW, D), vm(XN, KW, D), vm(KW, D), vm(ZN, KW, D), vm(KW, D), vm(GN, KW, D),
+            vm(2, 2 * D, ROWS, **b), vm(2, 2 * D, ROWS, **b), vm(D, ROWS, **b), vm(D, ROWS, **b),
+            vm(GN, KW, D), vm(GN, KW, D), vm(ROWS, D),
+            pltpu.SemaphoreType.DMA((10,)),
             pltpu.SemaphoreType.DMA((5, ZN)),
-            pltpu.SemaphoreType.DMA((9,)),
+            pltpu.SemaphoreType.DMA((10,)),
             pltpu.SemaphoreType.DMA((5, ZN)),
         ],
         compiler_params=pltpu.CompilerParams(
-            collective_id=0, has_side_effects=True, vmem_limit_bytes=48 * 1024 * 1024
+            collective_id=0, has_side_effects=True, vmem_limit_bytes=60 * 1024 * 1024
         ),
         cost_estimate=pl.CostEstimate(flops=3_000_000_000, bytes_accessed=2_500_000, transcendentals=400_000),
     )(queries, keys, values, cotangent, source_ids.reshape(1, ROWS), source_weights.reshape(1, -1), q_feature, k_feature)
+    return pl.pallas_call(
+        store,
+        out_shape=[jax.ShapeDtypeStruct(a.shape, a.dtype) for a in results],
+        in_specs=[pl.BlockSpec(memory_space=pl.ANY)] * 5,
+        out_specs=[pl.BlockSpec(memory_space=pl.ANY)] * 5,
+        scratch_shapes=[pltpu.SemaphoreType.DMA((5,))],
+    )(*results)
 
 
 def solution(mesh):

time: 86.4 us -> 97 us (1.12)
  Pallas kernels: 75.7 us -> 96.2 us
  local copies, waits for them, and re-layouts: 9.7 us -> 0 us
    pallas_call x0 -> x1, Pallas kernels: none -> 25 us  [on_device(): pl.pallas_call(store, out_shape=[jax.ShapeDtypeStruct(a.shape, a.dtype) f...]
    unnamed x21 -> x0, local copies, waits for them, and re-layouts: 9.7 us -> none
    pallas_call x1, Pallas kernels: 75.7 us -> 71.2 us  [on_device(): pl.pallas_call(kernel, out_shape=(jax.ShapeDtypeStruct((ROWS, 2 * D), F32...]
where the time goes in v2:
time: 97 us; the launch traced here: 96.8 us
  Pallas kernels  96.2 us (99%)
    pallas_call x1, Pallas kernels, on_device(): pl.pallas_call(kernel, out_shape=(jax.ShapeDtypeStruct((ROWS, 2 * D), F32...  71.2 us
    pallas_call x1, Pallas kernels, on_device(): pl.pallas_call(store, out_shape=[jax.ShapeDtypeStruct(a.shape, a.dtype) f...  25 us

profile of v2, /device:TPU:1, one launch (start us, length us, event | category | flops | bytes accessed | tf_op | source)
XLA Modules:
  0.0 96.8 jit_solution(15433457187248021529)
XLA Ops:
  0.6 71.2 %shard_map.119 = (f32[512,256]{1,0:T(8,128)}, f32[64,128]{1,0:T(8,128)}, f32[64,128]{1,0:T(8,128)}, f32[2,128,128]{2,1,0:T(8,128)}, f32[128,128]{1,0:T(8,128)}) custom-call(f32[512,256]{1,0:T(8,128)} %q_in.1, f32[512,128]{1,0:T(8,128)} %k_in.1, f32[512,128]{1,0:T(8,128)} %v_in.1, f32[512,256]{1,0:T(8,128)} %c_in.1, s32[1,512]{1,0:T(1,128)} %bitcast.2, ...), custom_call_target="tpu_custom_call" | custom-call | flops 3000000000 | bytes 2500000 | tf_op jit(solution)/shard_map/pallas_call | solution.py:459
  71.9 25.0 %shard_map.120 = (f32[512,256]{1,0:T(8,128)}, f32[64,128]{1,0:T(8,128)}, f32[64,128]{1,0:T(8,128)}, f32[2,128,128]{2,1,0:T(8,128)}, f32[128,128]{1,0:T(8,128)}) custom-call(f32[512,256]{1,0:T(8,128)} %get-tuple-element.10.refs_0_, f32[64,128]{1,0:T(8,128)} %get-tuple-element.11.refs_1_, f32[64,128]{1,0:T(8,128)} %get-tuple-element.12.refs_2_, ...), custom_call_target="tpu_custom_call" | custom-call | tf_op jit(solution)/shard_map/pallas_call | solution.py:499

commit v3 on v2

--- a/solution.py
+++ b/solution.py
@@ -127,6 +127,12 @@
     each_z(lambda zp: greet(zp * XN + x, h))
     each_group(lambda t, xp, hp: greet(z * XN + xp, hp))
 
+    pend = []
+
+    def finish():
+        for act in pend:
+            act()
+
     def start(src, dst, ssem, rsem, ctx, head):
         pltpu.make_async_remote_copy(
             src_ref=src, dst_ref=dst, send_sem=ssem, recv_sem=rsem,
@@ -139,12 +145,10 @@
     def send_group(src_of, dst, index):
         each_group(lambda t, xp, hp: start(
             src_of(t, xp, hp), dst.at[me], s_one.at[index], r_one.at[index], z * XN + xp, hp))
+        pend.append(lambda: drain(dst.at[pl.ds(0, GN - 1)], s_one.at[index]))
 
     def recv_group(dst, index):
         drain(dst.at[pl.ds(0, GN - 1)], r_one.at[index])
-
-    def sent_group(dst, index):
-        drain(dst.at[pl.ds(0, GN - 1)], s_one.at[index])
 
     def send_x(src_of, dst, index):
         def step(i, carry):
@@ -152,12 +156,10 @@
             start(src_of(xp), dst.at[x], s_one.at[index], r_one.at[index], z * XN + xp, h)
             return carry
         lax.fori_loop(0, XN - 1, step, 0)
+        pend.append(lambda: drain(dst.at[pl.ds(0, XN - 1)], s_one.at[index]))
 
     def recv_x(dst, index):
         drain(dst.at[pl.ds(0, XN - 1)], r_one.at[index])
-
-    def sent_x(dst, index):
-        drain(dst.at[pl.ds(0, XN - 1)], s_one.at[index])
 
     def send_z(src_of, dst, index, low, high):
         def act(zp):
@@ -165,6 +167,7 @@
             def _():
                 start(src_of(zp), dst.at[z], s_two.at[index, zp], r_two.at[index, z], zp * XN + x, h)
         each_z(act)
+        pend.append(lambda: wait_z(dst, s_two, index, low, high))
 
     def wait_z(dst, sems, index, low, high):
         def step(zp, carry):
@@ -341,6 +344,7 @@
         start(ks.at[hp], kr.at[h], s_one.at[5], r_one.at[5], pos, hp)
         return carry
     lax.fori_loop(1, HN, send_key, 0)
+    pend.append(lambda: drain(kr.at[pl.ds(0, HN - 1)], s_one.at[5]))
     kr[h] = ks[h]
     kpair = (kth[...], ktl[...])
     gkw = mm3(kpair, split(gl), NN)
@@ -423,32 +427,22 @@
         gkw_ref[KW * i:KW * i + KW, :] = gc[i]
     stores[4].start()
 
-    sent_x(ra.at[:, pl.ds(0, TM)], 0)
-    sent_group(ga, 1)
-    sent_group(rb.at[:, pl.ds(0, TM)], 2)
-    sent_x(rq, 3)
-    sent_group(gb, 4)
-    drain(kr.at[pl.ds(0, HN - 1)], s_one.at[5])
-    sent_x(rc, 6)
-    sent_group(ikr, 9)
-    sent_x(gx, 7)
-    sent_group(gc, 8)
-    wait_z(za.at[:, pl.ds(0, TM)], s_two, 0, z + 1, ZN)
-    wait_z(zb.at[:, pl.ds(0, TM)], s_two, 1, 0, z)
-    wait_z(zq, s_two, 2, 0, ZN)
-    wait_z(gz, s_two, 3, 0, ZN)
-    wait_z(zc, s_two, 4, 0, ZN)
     for copy in stores:
         copy.wait()
+    finish()
 
 
 def store(*refs):
-    sems = refs[10]
-    copies = [pltpu.make_async_copy(refs[i], refs[5 + i], sems.at[i]) for i in range(5)]
-    for copy in copies:
-        copy.start()
-    for copy in copies:
-        copy.wait()
+    sources, targets, held, sems = refs[:5], refs[5:10], refs[10:15], refs[15]
+    reads = [pltpu.make_async_copy(sources[i], held[i], sems.at[0, i]) for i in range(5)]
+    writes = [pltpu.make_async_copy(held[i], targets[i], sems.at[1, i]) for i in range(5)]
+    for read in reads:
+        read.start()
+    for read, write in zip(reads, writes):
+        read.wait()
+        write.start()
+    for write in writes:
+        write.wait()
 
 
 def on_device(queries, keys, values, cotangent, source_ids, source_weights, q_feature, k_feature):
@@ -501,7 +495,8 @@
         out_shape=[jax.ShapeDtypeStruct(a.shape, a.dtype) for a in results],
         in_specs=[pl.BlockSpec(memory_space=pl.ANY)] * 5,
         out_specs=[pl.BlockSpec(memory_space=pl.ANY)] * 5,
-        scratch_shapes=[pltpu.SemaphoreType.DMA((5,))],
+        scratch_shapes=[pltpu.VMEM(a.shape, a.dtype) for a in results] + [pltpu.SemaphoreType.DMA((2, 5))],
+        compiler_params=pltpu.CompilerParams(vmem_limit_bytes=60 * 1024 * 1024),
     )(*results)
 
 

time: 97 us -> 74.4 us (0.77)
  Pallas kernels: 96.2 us -> 73.6 us
    pallas_call x1, Pallas kernels: 25 us -> 2 us  [on_device(): pl.pallas_call(store, out_shape=[jax.ShapeDtypeStruct(a.shape, a.dtype) f...]
where the time goes in v3:
time: 74.4 us; the launch traced here: 74.3 us
  Pallas kernels  73.6 us (99%)
    pallas_call x1, Pallas kernels, on_device(): pl.pallas_call(kernel, out_shape=(jax.ShapeDtypeStruct((ROWS, 2 * D), F32...  71.6 us
    pallas_call x1, Pallas kernels, on_device(): pl.pallas_call(store, out_shape=[jax.ShapeDtypeStruct(a.shape, a.dtype) f...  2 us

profile of v3, /device:TPU:1, one launch (start us, length us, event | category | flops | bytes accessed | tf_op | source)
XLA Modules:
  0.0 74.3 jit_solution(18059410001635097452)
XLA Ops:
  0.6 71.6 %shard_map.119 = (f32[512,256]{1,0:T(8,128)}, f32[64,128]{1,0:T(8,128)}, f32[64,128]{1,0:T(8,128)}, f32[2,128,128]{2,1,0:T(8,128)}, f32[128,128]{1,0:T(8,128)}) custom-call(f32[512,256]{1,0:T(8,128)} %q_in.1, f32[512,128]{1,0:T(8,128)} %k_in.1, f32[512,128]{1,0:T(8,128)} %v_in.1, f32[512,256]{1,0:T(8,128)} %c_in.1, s32[1,512]{1,0:T(1,128)} %bitcast.2, ...), custom_call_target="tpu_custom_call" | custom-call | flops 3000000000 | bytes 2500000 | tf_op jit(solution)/shard_map/pallas_call | solution.py:453
  72.3 2.0 %shard_map.120 = (f32[512,256]{1,0:T(8,128)}, f32[64,128]{1,0:T(8,128)}, f32[64,128]{1,0:T(8,128)}, f32[2,128,128]{2,1,0:T(8,128)}, f32[128,128]{1,0:T(8,128)}) custom-call(f32[512,256]{1,0:T(8,128)} %get-tuple-element.10.refs_0_, f32[64,128]{1,0:T(8,128)} %get-tuple-element.11.refs_1_, f32[64,128]{1,0:T(8,128)} %get-tuple-element.12.refs_2_, ...), custom_call_target="tpu_custom_call" | custom-call | tf_op jit(solution)/shard_map/pallas_call | solution.py:493

commit v4 on v3

--- a/solution.py
+++ b/solution.py
@@ -318,8 +318,6 @@
             qs[parts * n + i] = gw[QX * i:QX * i + QX]
 
     after(0)
-    after(1)
-    stores[0].start()
     recv_group(rb.at[:, pl.ds(0, TM)], 2)
     by_x = []
     for i in range(XN):
@@ -329,6 +327,10 @@
         by_x.append(s)
     tb[...] = total(by_x)
     send_z(lambda zp: tb.at[pl.ds(0, TM)], zb.at[:, pl.ds(0, TM)], 1, 0, z)
+    after(1)
+    stores[0].start()
+    send_x(lambda xp: qs.at[xp], rq, 3)
+    rq[x] = qs[x]
 
     r = pl.ds(0, CH)
     cpair = split(c1[...])
@@ -339,21 +341,12 @@
         ks[i, :, :D] = gl[OWN * i:OWN * i + OWN]
         ks[i, :, D:] = gval[OWN * i:OWN * i + OWN, :]
 
-    def send_key(i, carry):
-        hp = (h + i) % HN
-        start(ks.at[hp], kr.at[h], s_one.at[5], r_one.at[5], pos, hp)
-        return carry
-    lax.fori_loop(1, HN, send_key, 0)
-    pend.append(lambda: drain(kr.at[pl.ds(0, HN - 1)], s_one.at[5]))
-    kr[h] = ks[h]
     kpair = (kth[...], ktl[...])
     gkw = mm3(kpair, split(gl), NN)
     for i in range(GN):
         iks[i] = gkw[KW * i:KW * i + KW]
     send_group(lambda t, xp, hp: iks.at[t], ikr, 9)
     ikr[me] = iks[me]
-    send_x(lambda xp: qs.at[xp], rq, 3)
-    rq[x] = qs[x]
 
     wait_z(zb.at[:, pl.ds(0, TM)], r_two, 1, z + 1, ZN)
     suf = jnp.sum(zb[...], axis=0)
@@ -386,6 +379,40 @@
     rc[x] = ck[me]
     gint[...] = gl
 
+    def send_key(i, carry):
+        hp = (h + i) % HN
+        start(ks.at[hp], kr.at[h], s_one.at[5], r_one.at[5], pos, hp)
+        return carry
+    lax.fori_loop(1, HN, send_key, 0)
+    pend.append(lambda: drain(kr.at[pl.ds(0, HN - 1)], s_one.at[5]))
+    kr[h] = ks[h]
+
+    wait_z(zq, r_two, 2, 0, ZN)
+    gzs[...] = jnp.sum(zq[...], axis=0)
+    send_z(lambda zp: gzs, gz, 3, 0, ZN)
+    gz[z] = gzs[...]
+
+    recv_x(rc, 6)
+    tc[...] = total(rc) + early
+    send_z(lambda zp: tc, zc, 4, 0, ZN)
+    zc[z] = tc[...]
+
+    wait_z(gz, r_two, 3, 0, ZN)
+    send_x(lambda xp: gz, gx, 7)
+    gx[x] = gz[...]
+
+    wait_z(zc, r_two, 4, 0, ZN)
+    gcs[...] = jnp.sum(zc[...], axis=0)
+    send_group(lambda t, xp, hp: gcs, gc, 8)
+    gc[me] = gcs[...]
+    last = pend.pop()
+
+    recv_x(gx, 7)
+    for i in range(XN):
+        for j in range(ZN):
+            row = QX * i + QZ * j
+            gqw_ref[row // D, row % D:row % D + QZ, :] = gx[i, j]
+    stores[3].start()
     own = pl.ds(h * OWN, OWN)
     drain(kr.at[pl.ds(0, HN - 1)], r_one.at[5])
     got = kr[0]
@@ -393,43 +420,16 @@
         got = got + kr[i]
     gk_ref[...] = mm3(split(gint[own, :] + got[:, :D]), split(kw_ref[...]), NT)
     gv_ref[...] = mm3((kh[own, :], kl[own, :]), later, NN) + got[:, D:]
-
     stores[1].start()
     stores[2].start()
-
-    recv_x(rc, 6)
-    tc[...] = total(rc) + early
-    send_z(lambda zp: tc, zc, 4, 0, ZN)
-    zc[z] = tc[...]
-
-    wait_z(zq, r_two, 2, 0, ZN)
-    gzs[...] = jnp.sum(zq[...], axis=0)
-    send_z(lambda zp: gzs, gz, 3, 0, ZN)
-    gz[z] = gzs[...]
-
-    wait_z(zc, r_two, 4, 0, ZN)
-    gcs[...] = jnp.sum(zc[...], axis=0)
-    send_group(lambda t, xp, hp: gcs, gc, 8)
-    gc[me] = gcs[...]
-
-    wait_z(gz, r_two, 3, 0, ZN)
-    send_x(lambda xp: gz, gx, 7)
-    gx[x] = gz[...]
-
-    recv_x(gx, 7)
-    for i in range(XN):
-        for j in range(ZN):
-            row = QX * i + QZ * j
-            gqw_ref[row // D, row % D:row % D + QZ, :] = gx[i, j]
-    stores[3].start()
+    finish()
     recv_group(gc, 8)
     for i in range(GN):
         gkw_ref[KW * i:KW * i + KW, :] = gc[i]
     stores[4].start()
-
+    last()
     for copy in stores:
         copy.wait()
-    finish()
 
 
 def store(*refs):

time: 74.4 us -> 73.8 us (level)
  no operation moved by 1% of the time
where the time goes in v4:
time: 73.8 us; the launch traced here: 73.7 us
  Pallas kernels  73.1 us (99%)
    pallas_call x1, Pallas kernels, on_device(): pl.pallas_call(kernel, out_shape=(jax.ShapeDtypeStruct((ROWS, 2 * D), F32...  71.1 us
    pallas_call x1, Pallas kernels, on_device(): pl.pallas_call(store, out_shape=[jax.ShapeDtypeStruct(a.shape, a.dtype) f...  2 us

profile of v4, /device:TPU:1, one launch (start us, length us, event | category | flops | bytes accessed | tf_op | source)
XLA Modules:
  0.0 73.7 jit_solution(11638056534354742554)
XLA Ops:
  0.6 71.1 %shard_map.119 = (f32[512,256]{1,0:T(8,128)}, f32[64,128]{1,0:T(8,128)}, f32[64,128]{1,0:T(8,128)}, f32[2,128,128]{2,1,0:T(8,128)}, f32[128,128]{1,0:T(8,128)}) custom-call(f32[512,256]{1,0:T(8,128)} %q_in.1, f32[512,128]{1,0:T(8,128)} %k_in.1, f32[512,128]{1,0:T(8,128)} %v_in.1, f32[512,256]{1,0:T(8,128)} %c_in.1, s32[1,512]{1,0:T(1,128)} %bitcast.2, ...), custom_call_target="tpu_custom_call" | custom-call | flops 3000000000 | bytes 2500000 | tf_op jit(solution)/shard_map/pallas_call | solution.py:453
  71.7 2.0 %shard_map.120 = (f32[512,256]{1,0:T(8,128)}, f32[64,128]{1,0:T(8,128)}, f32[64,128]{1,0:T(8,128)}, f32[2,128,128]{2,1,0:T(8,128)}, f32[128,128]{1,0:T(8,128)}) custom-call(f32[512,256]{1,0:T(8,128)} %get-tuple-element.10.refs_0_, f32[64,128]{1,0:T(8,128)} %get-tuple-element.11.refs_1_, f32[64,128]{1,0:T(8,128)} %get-tuple-element.12.refs_2_, ...), custom_call_target="tpu_custom_call" | custom-call | tf_op jit(solution)/shard_map/pallas_call | solution.py:493

commit v5 on v4

--- a/solution.py
+++ b/solution.py
@@ -79,7 +79,7 @@
     kf, kh, kl, vh, vl, qf, qh, ql, sh, sl, intra, scaled, st, gnh, gnl, gnorm, c1, gkf, gval,
     sa, ra, ta, za, gas, ga, cb, rb, tb, zb, gbs, gb, ks, kr, qs, rq, tq, zq, gzs, gz, gx, ck, rc, tc, zc, gcs, gc,
     qth, qtl, kth, ktl, iks, ikr, gint,
-    s_one, s_two, r_one, r_two,
+    s_one, s_two, r_one, r_two, ready,
 ):
     pos = lax.axis_index("ctx")
     h = lax.axis_index("head")
@@ -124,8 +124,28 @@
     ]
     za[...] = jnp.zeros_like(za)
     zb[...] = jnp.zeros_like(zb)
-    each_z(lambda zp: greet(zp * XN + x, h))
-    each_group(lambda t, xp, hp: greet(z * XN + xp, hp))
+    core = h % 2
+    first = h - core
+
+    def greet_x(i, carry):
+        greet(z * XN + (x + swing(i, XN)) % XN, first)
+        return carry
+    lax.fori_loop(0, XN - 1, greet_x, 0)
+
+    @pl.when(core == 1)
+    def _():
+        greet(pos, first)
+    each_z(lambda zp: greet(zp * XN + x, first + 1))
+
+    def greet_chip(i, carry):
+        yp = (h // 2 + swing(i % (HN // 2), HN // 2)) % (HN // 2)
+        greet(z * XN + (x + swing(i // (HN // 2), XN)) % XN, yp * 2 + 1)
+        return carry
+    lax.fori_loop(0, GN // 2 - 1, greet_chip, 0)
+
+    @pl.when(core == 0)
+    def _():
+        greet(pos, first + 1)
 
     pend = []
 
@@ -197,7 +217,14 @@
     for i in range(XN):
         sa[i, :TR] = mine[TR * i:TR * i + TR]
         sa[i, TR:TM] = tot_all
-    pl.semaphore_wait(barrier, GN - 1 + ZN - 1)
+    @pl.when(core == 0)
+    def _():
+        pl.semaphore_wait(barrier, 2 * (XN - 1) + 1)
+        pl.semaphore_signal(ready.at[0], inc=1, device_id=(pos, first + 1), device_id_type=MESH)
+
+    @pl.when(core == 1)
+    def _():
+        pl.semaphore_wait(ready.at[0], 1)
     send_x(lambda xp: sa.at[xp, pl.ds(0, TM)], ra.at[:, pl.ds(0, TM)], 0)
     ra[x] = sa[x]
 
@@ -229,6 +256,14 @@
             sh[n, r, :], sl[n, r, :] = split(jnp.where(mask, s, 0.0))
             intra[n, r, :] = mm3((sh[n, r, :], sl[n, r, :]), (vh[r, :], vl[r, :]), NN)
 
+    @pl.when(core == 1)
+    def _():
+        pl.semaphore_wait(barrier, 2 * (ZN - 1) + GN - 1)
+        pl.semaphore_signal(ready.at[1], inc=1, device_id=(pos, first), device_id_type=MESH)
+
+    @pl.when(core == 0)
+    def _():
+        pl.semaphore_wait(ready.at[1], 1)
     recv_x(ra.at[:, pl.ds(0, TM)], 0)
     ta[...] = total(ra)
     send_z(lambda zp: ta.at[pl.ds(0, TM)], za.at[:, pl.ds(0, TM)], 0, z + 1, ZN)
@@ -286,12 +321,12 @@
     send_group(lambda t, xp, hp: cb.at[t, pl.ds(0, TM)], rb.at[:, pl.ds(0, TM)], 2)
     rb[me] = cb[me]
 
-    def after(n):
+    grads = [[], []]
+
+    def after(n, parts):
         lanes = pl.ds(n * D, D)
         wpair = split(qw_ref[n])
-        xs = split(q_ref[:, lanes])
-        grads = []
-        for c in range(NC):
+        for c in parts:
             r = pl.ds(c * CH, CH)
             g = (gnh[n, r, :], gnl[n, r, :])
             gno = gnorm[n, r, :]
@@ -301,7 +336,7 @@
             a = gfeat[:, :D] + gno * totals[c][0]
             b = gfeat[:, D:] + gno * totals[c][1]
             gl = split(back(qf[n, r, :D], qf[n, r, D:], a, b))
-            grads.append(gl)
+            grads[n].append(gl)
             gq_ref[r, lanes] = mm3(gl, wpair, NT)
             gk = mm3(gs, (qh[n, r, :], ql[n, r, :]), TN)
             gv = mm3((sh[n, r, :], sl[n, r, :]), g, TN)
@@ -311,13 +346,17 @@
             else:
                 gkf[r, :] += gk
                 gval[r, :] += gv
-        gl = (jnp.concatenate([g[0] for g in grads], axis=0), jnp.concatenate([g[1] for g in grads], axis=0))
-        gw = mm3(xs, gl, TN)
+
+    def weight_grad(n):
+        gl = tuple(jnp.concatenate([g[i] for g in grads[n]], axis=0) for i in range(2))
+        gw = mm3(split(q_ref[:, n * D:n * D + D]), gl, TN)
         parts = XN // 2
         for i in range(parts):
             qs[parts * n + i] = gw[QX * i:QX * i + QX]
 
-    after(0)
+    after(0, (0, 1))
+    weight_grad(0)
+    after(1, (0,))
     recv_group(rb.at[:, pl.ds(0, TM)], 2)
     by_x = []
     for i in range(XN):
@@ -327,7 +366,8 @@
         by_x.append(s)
     tb[...] = total(by_x)
     send_z(lambda zp: tb.at[pl.ds(0, TM)], zb.at[:, pl.ds(0, TM)], 1, 0, z)
-    after(1)
+    after(1, (1,))
+    weight_grad(1)
     stores[0].start()
     send_x(lambda xp: qs.at[xp], rq, 3)
     rq[x] = qs[x]
@@ -484,6 +524,7 @@
             pltpu.SemaphoreType.DMA((5, ZN)),
             pltpu.SemaphoreType.DMA((10,)),
             pltpu.SemaphoreType.DMA((5, ZN)),
+            pltpu.SemaphoreType.REGULAR((2,)),
         ],
         compiler_params=pltpu.CompilerParams(
             collective_id=0, has_side_effects=True, vmem_limit_bytes=60 * 1024 * 1024

time: 73.8 us -> 71.6 us (0.970)
  Pallas kernels: 73.1 us -> 70.8 us
    pallas_call x1, Pallas kernels: 71.1 us -> 68.8 us  [on_device(): pl.pallas_call(kernel, out_shape=(jax.ShapeDtypeStruct((ROWS, 2 * D), F32...]
where the time goes in v5:
time: 71.6 us; the launch traced here: 71.4 us
  Pallas kernels  70.8 us (99%)
    pallas_call x1, Pallas kernels, on_device(): pl.pallas_call(kernel, out_shape=(jax.ShapeDtypeStruct((ROWS, 2 * D), F32...  68.8 us
    pallas_call x1, Pallas kernels, on_device(): pl.pallas_call(store, out_shape=[jax.ShapeDtypeStruct(a.shape, a.dtype) f...  2 us

profile of v5, /device:TPU:1, one launch (start us, length us, event | category | flops | bytes accessed | tf_op | source)
XLA Modules:
  0.0 71.4 jit_solution(9541502192866389910)
XLA Ops:
  0.6 68.8 %shard_map.119 = (f32[512,256]{1,0:T(8,128)}, f32[64,128]{1,0:T(8,128)}, f32[64,128]{1,0:T(8,128)}, f32[2,128,128]{2,1,0:T(8,128)}, f32[128,128]{1,0:T(8,128)}) custom-call(f32[512,256]{1,0:T(8,128)} %q_in.1, f32[512,128]{1,0:T(8,128)} %k_in.1, f32[512,128]{1,0:T(8,128)} %v_in.1, f32[512,256]{1,0:T(8,128)} %c_in.1, s32[1,512]{1,0:T(1,128)} %bitcast.2, ...), custom_call_target="tpu_custom_call" | custom-call | flops 3000000000 | bytes 2500000 | tf_op jit(solution)/shard_map/pallas_call | solution.py:493
  69.4 2.0 %shard_map.120 = (f32[512,256]{1,0:T(8,128)}, f32[64,128]{1,0:T(8,128)}, f32[64,128]{1,0:T(8,128)}, f32[2,128,128]{2,1,0:T(8,128)}, f32[128,128]{1,0:T(8,128)}) custom-call(f32[512,256]{1,0:T(8,128)} %get-tuple-element.10.refs_0_, f32[64,128]{1,0:T(8,128)} %get-tuple-element.11.refs_1_, f32[64,128]{1,0:T(8,128)} %get-tuple-element.12.refs_2_, ...), custom_call_target="tpu_custom_call" | custom-call | tf_op jit(solution)/shard_map/pallas_call | solution.py:534

commit v6 on v5

--- a/solution.py
+++ b/solution.py
@@ -78,7 +78,7 @@
     q_ref, k_ref, v_ref, c_ref, ids_ref, sw_ref, qw_ref, kw_ref, i_sem,
     kf, kh, kl, vh, vl, qf, qh, ql, sh, sl, intra, scaled, st, gnh, gnl, gnorm, c1, gkf, gval,
     sa, ra, ta, za, gas, ga, cb, rb, tb, zb, gbs, gb, ks, kr, qs, rq, tq, zq, gzs, gz, gx, ck, rc, tc, zc, gcs, gc,
-    qth, qtl, kth, ktl, iks, ikr, gint,
+    qth, qtl, kth, ktl, iks, ikr, gint, invs, ctb, ctr, ctt, zct,
     s_one, s_two, r_one, r_two, ready,
 ):
     pos = lax.axis_index("ctx")
@@ -124,6 +124,7 @@
     ]
     za[...] = jnp.zeros_like(za)
     zb[...] = jnp.zeros_like(zb)
+    zct[...] = jnp.zeros_like(zct)
     core = h % 2
     first = h - core
 
@@ -268,6 +269,7 @@
     ta[...] = total(ra)
     send_z(lambda zp: ta.at[pl.ds(0, TM)], za.at[:, pl.ds(0, TM)], 0, z + 1, ZN)
     before(0)
+    before(1)
     wait_z(za.at[:, pl.ds(0, TM)], r_two, 0, 0, z)
     pre = jnp.sum(za[...], axis=0)
     pre_tot = pre[TR:TM]
@@ -278,48 +280,50 @@
             pre_tot = pre_tot + jnp.where(i < x, ra[i, TR:TM], 0.0)
     send_group(lambda t, xp, hp: gas.at[xp], ga, 1)
     ga[me] = gas[x]
-    before(1)
-    recv_group(ga, 1)
-
-    p_now = ga[...].reshape(2 * D, D)
-    tot_now = (pre_tot[0:1], pre_tot[1:2])
-    states, totals = [], []
-    for c in range(NC):
-        states.append(split(p_now))
-        totals.append(tot_now)
-        if c < NC - 1:
-            p_now = p_now + st[c]
-            tot_now = (tot_now[0] + tot[c][0], tot_now[1] + tot[c][1])
-    ct = [[0.0, 0.0] for _ in range(NC)]
+
+    totals = [(pre_tot[0:1], pre_tot[1:2])]
+    for c in range(1, NC):
+        totals.append((totals[c - 1][0] + tot[c - 1][0], totals[c - 1][1] + tot[c - 1][1]))
     carried = []
     for c in range(NC):
         r = pl.ds(c * CH, CH)
-        thi, tlo = split(jnp.concatenate([column(totals[c][0]), column(totals[c][1])], axis=0))
-        full = (jnp.concatenate([states[c][0], thi], axis=1), jnp.concatenate([states[c][1], tlo], axis=1))
+        col = split(jnp.concatenate([column(totals[c][0]), column(totals[c][1])], axis=0))
         acc = None
         for n in range(2):
-            q = (qh[n, r, :], ql[n, r, :])
-            nn = intra[n, r, :] + mm3(q, full, NN)
-            inv = 1.0 / nn[:, D:]
-            sc = scaled[n, r, :]
-            gnum = sc * inv
-            gno = -jnp.sum(sc * (nn[:, :D] * inv), axis=1, keepdims=True) * inv
-            gnorm[n, r, :] = gno
-            g = split(gnum)
+            inv = 1.0 / (intra[n, r, D:] + mm3((qh[n, r, :], ql[n, r, :]), col, NN))
+            invs[n, r, :] = inv
+            g = split(scaled[n, r, :] * inv)
             gnh[n, r, :], gnl[n, r, :] = g
-            ct[c][0] = ct[c][0] + jnp.sum(gno * qf[n, r, :D], axis=0, keepdims=True)
-            ct[c][1] = ct[c][1] + jnp.sum(gno * qf[n, r, D:], axis=0, keepdims=True)
             term = mm3((qth[n, :, r], qtl[n, :, r]), g, NN)
             acc = term if acc is None else acc + term
         carried.append(acc)
     c1[...] = carried[1]
     whole = carried[0] + carried[1]
-    ct_all = jnp.concatenate([ct[0][0] + ct[1][0], ct[0][1] + ct[1][1]], axis=0)
     for t in range(GN):
-        cb[t, :TR] = whole[TR * t:TR * t + TR]
-        cb[t, TR:TM] = ct_all
-    send_group(lambda t, xp, hp: cb.at[t, pl.ds(0, TM)], rb.at[:, pl.ds(0, TM)], 2)
+        cb[t] = whole[TR * t:TR * t + TR]
+    send_group(lambda t, xp, hp: cb.at[t], rb, 2)
     rb[me] = cb[me]
+
+    recv_group(ga, 1)
+    p_now = ga[...].reshape(2 * D, D)
+    states = []
+    for c in range(NC):
+        states.append(split(p_now))
+        if c < NC - 1:
+            p_now = p_now + st[c]
+    ct = [[0.0, 0.0] for _ in range(NC)]
+    for c in range(NC):
+        r = pl.ds(c * CH, CH)
+        for n in range(2):
+            num = intra[n, r, :D] + mm3((qh[n, r, :], ql[n, r, :]), states[c], NN)
+            inv = invs[n, r, :]
+            gno = -jnp.sum(scaled[n, r, :] * (num * inv), axis=1, keepdims=True) * inv
+            gnorm[n, r, :] = gno
+            ct[c][0] = ct[c][0] + jnp.sum(gno * qf[n, r, :D], axis=0, keepdims=True)
+            ct[c][1] = ct[c][1] + jnp.sum(gno * qf[n, r, D:], axis=0, keepdims=True)
+    ctb[...] = jnp.concatenate([ct[0][0] + ct[1][0], ct[0][1] + ct[1][1]], axis=0)
+    send_group(lambda t, xp, hp: ctb, ctr, 10)
+    ctr[me] = ctb[...]
 
     grads = [[], []]
 
@@ -354,21 +358,38 @@
         for i in range(parts):
             qs[parts * n + i] = gw[QX * i:QX * i + QX]
 
+    def over_heads(ref):
+        sums = []
+        for i in range(XN):
+            acc = ref[i]
+            for hp in range(1, HN):
+                acc = acc + ref[hp * XN + i]
+            sums.append(acc)
+        return sums
+
+    recv_group(rb, 2)
+    by_x = over_heads(rb)
+    tb[...] = total(by_x)
+    send_z(lambda zp: tb, zb, 1, 0, z)
     after(0, (0, 1))
+    after(1, (0,))
+    recv_group(ctr, 10)
+    ct_x = over_heads(ctr)
+    ctt[...] = total(ct_x)
+    send_z(lambda zp: ctt, zct, 5, 0, z)
+    after(1, (1,))
+    stores[0].start()
+
+    wait_z(zb, r_two, 1, z + 1, ZN)
+    suf = jnp.sum(zb[...], axis=0)
+    for i in reversed(range(XN)):
+        gbs[i] = suf
+        if i > 0:
+            suf = suf + by_x[i]
+    send_group(lambda t, xp, hp: gbs.at[xp], gb, 4)
+    gb[me] = gbs[x]
     weight_grad(0)
-    after(1, (0,))
-    recv_group(rb.at[:, pl.ds(0, TM)], 2)
-    by_x = []
-    for i in range(XN):
-        s = rb[i]
-        for hp in range(1, HN):
-            s = s + rb[hp * XN + i]
-        by_x.append(s)
-    tb[...] = total(by_x)
-    send_z(lambda zp: tb.at[pl.ds(0, TM)], zb.at[:, pl.ds(0, TM)], 1, 0, z)
-    after(1, (1,))
     weight_grad(1)
-    stores[0].start()
     send_x(lambda xp: qs.at[xp], rq, 3)
     rq[x] = qs[x]
 
@@ -388,17 +409,6 @@
     send_group(lambda t, xp, hp: iks.at[t], ikr, 9)
     ikr[me] = iks[me]
 
-    wait_z(zb.at[:, pl.ds(0, TM)], r_two, 1, z + 1, ZN)
-    suf = jnp.sum(zb[...], axis=0)
-    suf_tot = suf[TR:TM]
-    for i in reversed(range(XN)):
-        gbs[i] = suf[:TR]
-        if i > 0:
-            suf = suf + by_x[i]
-            suf_tot = suf_tot + jnp.where(i > x, by_x[i][TR:TM], 0.0)
-    send_group(lambda t, xp, hp: gbs.at[xp], gb, 4)
-    gb[me] = gbs[x]
-
     recv_x(rq, 3)
     tsum = total(rq)
     for i in range(ZN):
@@ -409,6 +419,10 @@
     early = jnp.sum(ikr[...], axis=0)
 
     recv_group(gb, 4)
+    wait_z(zct, r_two, 5, z + 1, ZN)
+    suf_tot = jnp.sum(zct[...], axis=0)
+    for i in range(1, XN):
+        suf_tot = suf_tot + jnp.where(i > x, ct_x[i], 0.0)
     later = split(gb[...].reshape(2 * D, D))
     gfeat = mm3((vh[:, :D], vl[:, :D]), later, NT)
     gl = back(kf[:, :D], kf[:, D:], gfeat[:, :D] + suf_tot[0:1], gfeat[:, D:] + suf_tot[1:2])
@@ -513,17 +527,18 @@
             vm(2, ROWS, D, **b), vm(2, ROWS, D, **b), vm(2, ROWS, D),
             vm(2 * D, D), vm(ROWS, 2 * D), vm(ROWS, D),
             vm(XN, TP, D), vm(XN, TP, D), vm(TP, D), vm(ZN, TP, D), vm(XN, TR, D), vm(GN, TR, D),
-            vm(GN, TP, D), vm(GN, TP, D), vm(TP, D), vm(ZN, TP, D), vm(XN, TR, D), vm(GN, TR, D),
+            vm(GN, TR, D), vm(GN, TR, D), vm(TR, D), vm(ZN, TR, D), vm(XN, TR, D), vm(GN, TR, D),
             vm(HN, OWN, 2 * D), vm(HN, OWN, 2 * D),
             vm(XN, QX, D), vm(XN, QX, D), vm(ZN, QZ, D), vm(ZN, QZ, D),
             vm(QZ, D), vm(ZN, QZ, D), vm(XN, ZN, QZ, D),
             vm(GN, KW, D), vm(XN, KW, D), vm(KW, D), vm(ZN, KW, D), vm(KW, D), vm(GN, KW, D),
             vm(2, 2 * D, ROWS, **b), vm(2, 2 * D, ROWS, **b), vm(D, ROWS, **b), vm(D, ROWS, **b),
             vm(GN, KW, D), vm(GN, KW, D), vm(ROWS, D),
-            pltpu.SemaphoreType.DMA((10,)),
-            pltpu.SemaphoreType.DMA((5, ZN)),
-            pltpu.SemaphoreType.DMA((10,)),
-            pltpu.SemaphoreType.DMA((5, ZN)),
+            vm(2, ROWS, D), vm(2, D), vm(GN, 2, D), vm(2, D), vm(ZN, 2, D),
+            pltpu.SemaphoreType.DMA((11,)),
+            pltpu.SemaphoreType.DMA((6, ZN)),
+            pltpu.SemaphoreType.DMA((11,)),
+            pltpu.SemaphoreType.DMA((6, ZN)),
             pltpu.SemaphoreType.REGULAR((2,)),
         ],
         compiler_params=pltpu.CompilerParams(

time: 71.6 us -> 72.4 us (1.011)
  Pallas kernels: 70.8 us -> 71.6 us
    pallas_call x1, Pallas kernels: 68.8 us -> 69.6 us  [on_device(): pl.pallas_call(kernel, out_shape=(jax.ShapeDtypeStruct((ROWS, 2 * D), F32...]
where the time goes in v6:
time: 72.4 us; the launch traced here: 72.2 us
  Pallas kernels  71.6 us (99%)
    pallas_call x1, Pallas kernels, on_device(): pl.pallas_call(kernel, out_shape=(jax.ShapeDtypeStruct((ROWS, 2 * D), F32...  69.6 us
    pallas_call x1, Pallas kernels, on_device(): pl.pallas_call(store, out_shape=[jax.ShapeDtypeStruct(a.shape, a.dtype) f...  2 us

profile of v6, /device:TPU:1, one launch (start us, length us, event | category | flops | bytes accessed | tf_op | source)
XLA Modules:
  0.0 72.2 jit_solution(17670325051730801594)
XLA Ops:
  0.6 69.6 %shard_map.119 = (f32[512,256]{1,0:T(8,128)}, f32[64,128]{1,0:T(8,128)}, f32[64,128]{1,0:T(8,128)}, f32[2,128,128]{2,1,0:T(8,128)}, f32[128,128]{1,0:T(8,128)}) custom-call(f32[512,256]{1,0:T(8,128)} %q_in.1, f32[512,128]{1,0:T(8,128)} %k_in.1, f32[512,128]{1,0:T(8,128)} %v_in.1, f32[512,256]{1,0:T(8,128)} %c_in.1, s32[1,512]{1,0:T(1,128)} %bitcast.2, ...), custom_call_target="tpu_custom_call" | custom-call | flops 3000000000 | bytes 2500000 | tf_op jit(solution)/shard_map/pallas_call | solution.py:507
  70.2 2.0 %shard_map.120 = (f32[512,256]{1,0:T(8,128)}, f32[64,128]{1,0:T(8,128)}, f32[64,128]{1,0:T(8,128)}, f32[2,128,128]{2,1,0:T(8,128)}, f32[128,128]{1,0:T(8,128)}) custom-call(f32[512,256]{1,0:T(8,128)} %get-tuple-element.10.refs_0_, f32[64,128]{1,0:T(8,128)} %get-tuple-element.11.refs_1_, f32[64,128]{1,0:T(8,128)} %get-tuple-element.12.refs_2_, ...), custom_call_target="tpu_custom_call" | custom-call | tf_op jit(solution)/shard_map/pallas_call | solution.py:549
